TPU v7x, 32 devices: a whole 2x2x4 slice. The times are simulated.
32 devices in a mesh: parts: 2 (over x), space: 8 (over z, y), chan: 2 (over core).
Axes of the slice: x: 2, y: 2, z: 4, core: 2. Of those that a mesh axis runs over, the one named last changes fastest.
Arguments:
- field: bfloat16 [192, 768, 256], P(('parts', 'space'), None, 'chan'), parts along dimension 0, may hold values from -6 to 6
- spectral_weight: bfloat16 [96, 256, 256], P('space', None, 'chan'), may hold values from -5 to 5
- cotangent: bfloat16 [192, 768, 256], P(('parts', 'space'), None, 'chan'), parts along dimension 0, may hold values from -6 to 6
Outputs:
- output: bfloat16 [192, 768, 256], P(('parts', 'space'), None, 'chan'), parts along dimension 0
- field_grad: bfloat16 [192, 768, 256], P(('parts', 'space'), None, 'chan'), parts along dimension 0
- weight_grad: bfloat16 [192, 256, 256], P(('parts', 'space'), None, 'chan'), parts along dimension 0
There are 2 independent parts, one for each index of `parts`. A program takes and returns all parts, laid end to end along the dimension named above; an argument that names none is the same for every part. Nothing has to cross between parts.
All inputs are finite; a program needn't handle non-finite values.
Results may differ from a plain program's by a relative error of at most 0.02.
Values may be sent and summed in bfloat16 or wider, within the bound.
A program may use at most 128 MiB of HBM per device.

v0:
```python
import math

import jax
import jax.numpy as jnp
from jax import lax
from jax.sharding import PartitionSpec as P

CH = 256
DEG_DEV = 12


LIMIT = 2.0**40
SHRINK = 2.0 ** (-40)
LOGSTEP = 40.0 * math.log(2.0)


def legendre(order_ints, cosines, sine_values, degrees):
    orders = order_ints.astype(jnp.float32)
    order_col = orders[:, None]
    log_start = (
        0.5
        * (
            jnp.log((2.0 * order_col + 1.0) / (4.0 * math.pi))
            + lax.lgamma(order_col + 0.5)
            - lax.lgamma(order_col + 1.0)
            - 0.5 * math.log(math.pi)
        )
        + order_col * jnp.log(sine_values)[None, :]
    )
    state_shape = (orders.shape[0], cosines.shape[0])
    degree_list = jnp.arange(degrees).astype(jnp.float32)
    degree_col = degree_list[:, None]
    order_row = orders[None, :]
    upper_all = jnp.sqrt(
        (4.0 * degree_col * degree_col - 1.0)
        / jnp.maximum(degree_col * degree_col - order_row * order_row, 1.0)
    )
    lower_deg = degree_col - 1.0
    lower_all = jnp.sqrt(
        jnp.maximum(lower_deg * lower_deg - order_row * order_row, 0.0)
        / jnp.maximum(4.0 * lower_deg * lower_deg - 1.0, 1.0)
    )

    def advance(state_now, inputs):
        previous, before, rescales = state_now
        degree, upper_row, lower_row = inputs
        upper_coef = upper_row[:, None]
        lower_coef = lower_row[:, None]
        newest = jnp.where(
            degree == order_col,
            1.0,
            jnp.where(
                degree > order_col,
                upper_coef * (cosines[None, :] * previous - lower_coef * before),
                0.0,
            ),
        )
        too_large = jnp.abs(newest) > LIMIT
        newest = jnp.where(too_large, newest * SHRINK, newest)
        previous = jnp.where(too_large, previous * SHRINK, previous)
        rescales = rescales + too_large.astype(jnp.float32)
        return ((newest, previous, rescales), newest * jnp.exp(log_start + rescales * LOGSTEP))

    zero_state = jnp.zeros(state_shape, jnp.float32)
    final_state, values = lax.scan(
        advance,
        (zero_state, zero_state, zero_state),
        (degree_list, upper_all, lower_all),
        unroll=16,
    )
    return jnp.transpose(values, (1, 2, 0))


def spectral_tables(order_ints, latitudes, longitudes, degrees):
    half_lats = latitudes // 2
    latitude = (jnp.arange(latitudes).astype(jnp.float32) + 0.5) * (math.pi / latitudes)
    sine_values = jnp.sin(latitude)
    north_angle = latitude[:half_lats]
    north = legendre(order_ints, jnp.cos(north_angle), jnp.sin(north_angle), degrees)
    parity = (order_ints[:, None] + jnp.arange(degrees, dtype=jnp.int32)[None, :]) % 2
    signs = (1 - 2 * parity).astype(jnp.float32)
    south = signs[:, None, :] * north[:, ::-1, :]
    base_values = jnp.concatenate([north, south], axis=1)
    quadrature = math.pi**1.5 / math.sqrt(latitudes * longitudes) * sine_values
    analysis = quadrature[None, :, None] * base_values
    synthesis = math.sqrt(4.0 * math.pi / (latitudes * longitudes)) * base_values
    return (analysis, synthesis)


def fourier_table(longitudes, order_total):
    columns = (
        jnp.arange(longitudes, dtype=jnp.int32)[:, None]
        * jnp.arange(order_total, dtype=jnp.int32)[None, :]
    )
    phase_angle = 2.0 * math.pi / longitudes * (columns % longitudes).astype(jnp.float32)
    columns_table = jnp.stack([jnp.cos(phase_angle), -jnp.sin(phase_angle)], axis=2)
    return columns_table.reshape(longitudes, 2 * order_total)


def order_weights(order_total):
    return jnp.repeat(jnp.where(jnp.arange(order_total) == 0, 1.0, 2.0), 2).astype(jnp.float32)


def into_orders(values):
    return lax.all_to_all(values, "space", split_axis=1, concat_axis=0, tiled=True)


def into_degrees(values):
    return lax.all_to_all(values, "space", split_axis=1, concat_axis=0, tiled=True)


def from_degrees(values):
    return lax.all_to_all(values, "space", split_axis=0, concat_axis=1, tiled=True)


def into_latitudes(values):
    return lax.all_to_all(values, "space", split_axis=0, concat_axis=1, tiled=True)


def local(field, spectral_weight, cotangent):
    spaces = lax.axis_size("space")
    local_lats, longitudes, half_width = field.shape
    latitudes = local_lats * spaces
    degree_total = DEG_DEV * spaces
    mix_scale = 1.0 / math.sqrt(CH)
    forward_table = fourier_table(longitudes, degree_total)
    forward_cast = forward_table.astype(jnp.bfloat16)
    inverse_cast = (forward_table * order_weights(degree_total)[None, :]).T.astype(jnp.bfloat16)
    my_orders = lax.axis_index("space") * DEG_DEV + jnp.arange(DEG_DEV, dtype=jnp.int32)
    analysis_wide, synthesis_wide = spectral_tables(my_orders, latitudes, longitudes, degree_total)
    analysis = analysis_wide.astype(jnp.bfloat16)
    synthesis = synthesis_wide.astype(jnp.bfloat16)
    fourier = jnp.einsum(
        "jkc,kn->jnc", field, forward_cast, preferred_element_type=jnp.float32
    ).astype(jnp.bfloat16)
    by_order = into_orders(fourier).reshape(latitudes, DEG_DEV, 2, half_width)
    coeffs = jnp.einsum(
        "mjl,jmrc->mlrc", analysis, by_order, preferred_element_type=jnp.float32
    ).astype(jnp.bfloat16)
    by_degree = into_degrees(coeffs)
    all_channels = lax.all_gather(by_degree, "chan", axis=3, tiled=True)
    mixed_coef = (
        jnp.einsum(
            "mlrc,lco->mlro", all_channels, spectral_weight, preferred_element_type=jnp.float32
        )
        * mix_scale
    ).astype(jnp.bfloat16)
    mixed_orders = from_degrees(mixed_coef)
    grid_values = jnp.einsum(
        "mjl,mlrc->jmrc", synthesis, mixed_orders, preferred_element_type=jnp.float32
    ).astype(jnp.bfloat16)
    grid_band = into_latitudes(grid_values.reshape(latitudes, 2 * DEG_DEV, half_width))
    response = jnp.einsum(
        "jnc,nk->jkc", grid_band, inverse_cast, preferred_element_type=jnp.float32
    )
    normal_cdf = 0.5 * (1.0 + lax.erf(response * (1.0 / math.sqrt(2.0))))
    output = (field.astype(jnp.float32) + response * normal_cdf).astype(jnp.bfloat16)
    density = jnp.exp(-0.5 * response * response) * (1.0 / math.sqrt(2.0 * math.pi))
    response_grad = (cotangent.astype(jnp.float32) * (normal_cdf + response * density)).astype(
        jnp.bfloat16
    )
    grid_grad = jnp.einsum(
        "jkc,nk->jnc", response_grad, inverse_cast, preferred_element_type=jnp.float32
    ).astype(jnp.bfloat16)
    grad_by_order = into_orders(grid_grad).reshape(latitudes, DEG_DEV, 2, half_width)
    mixed_grad = jnp.einsum(
        "mjl,jmrc->mlrc", synthesis, grad_by_order, preferred_element_type=jnp.float32
    ).astype(jnp.bfloat16)
    grad_by_degree = into_degrees(mixed_grad)
    weight_grad = (
        jnp.einsum(
            "mlrc,mlro->lco", all_channels, grad_by_degree, preferred_element_type=jnp.float32
        )
        * mix_scale
    ).astype(jnp.bfloat16)
    partial_terms = jnp.einsum(
        "mlro,lco->mlrc", grad_by_degree, spectral_weight, preferred_element_type=jnp.float32
    )
    coeff_grad = (
        lax.psum_scatter(
            partial_terms.astype(jnp.bfloat16), "chan", scatter_dimension=3, tiled=True
        ).astype(jnp.float32)
        * mix_scale
    ).astype(jnp.bfloat16)
    coeff_orders = from_degrees(coeff_grad)
    fourier_grad = jnp.einsum(
        "mjl,mlrc->jmrc", analysis, coeff_orders, preferred_element_type=jnp.float32
    ).astype(jnp.bfloat16)
    fourier_band = into_latitudes(fourier_grad.reshape(latitudes, 2 * DEG_DEV, half_width))
    field_grad = (
        cotangent.astype(jnp.float32)
        + jnp.einsum("jnc,kn->jkc", fourier_band, forward_cast, preferred_element_type=jnp.float32)
    ).astype(jnp.bfloat16)
    return (output, field_grad, weight_grad)


def solution(mesh):
    in_specs = (
        P(("parts", "space"), None, "chan"),
        P("space", None, "chan"),
        P(("parts", "space"), None, "chan"),
    )
    out_specs = (
        P(("parts", "space"), None, "chan"),
        P(("parts", "space"), None, "chan"),
        P(("parts", "space"), None, "chan"),
    )
    return jax.shard_map(local, mesh=mesh, in_specs=in_specs, out_specs=out_specs, check_vma=False)
```

profile of v0, /device:TPU:8, one launch (start us, length us, event | category | flops | bytes accessed | tf_op | source)
XLA Modules:
  0.0 313.7 jit_solution(16415281105642627320)
XLA Ops:
  7.2 1.2 sine_negate_fusion
  9.3 1.3 copy.131
  10.6 2.3 reshape.813
  12.8 1.7 fusion.183
  14.5 1.3 copy.134
  15.8 6.3 %all-to-all-start = ((bf16[12,192,128]{2,0,1:T(8,128)(2,1)}), bf16[12,192,128]{2,0,1:T(8,128)(2,1)}, u32[]{:S(2)}, u32[]{:S(2)}) async-start(bf16[12,192,128]{2,0,1:T(8,128)(2,1)} %copy.134), calls=%async_computation | async-start | bytes 1572864 | tf_op jit(solution)/shard_map/all_to_all | solution.py:105
  22.5 82.7 %while.18 = (s32[]{:T(128)}, f32[12,48]{1,0:T(8,128)S(1)}, f32[12,48]{1,0:T(8,128)S(1)}, f32[12,48]{1,0:T(8,128)S(1)}, f32[6,16,12,48]{3,2,1,0:T(8,128)}, /*inde...) while((s32[]{:T(128)}, f32[12,48]{1,0:T(8,128)S(1)}, ...), condition=%wide.region_1.2_spmd.clone.clone, body=%wide.region_0.1_spmd.clone.clone.sunk | while | flops 499025 | bytes 916854 | solution.py:65
  22.5 0.7 fusion.260
  25.0 0.7 compare_bitcast_fusion.51
  36.3 0.7 fusion.260
  38.8 0.7 compare_bitcast_fusion.51
  50.0 0.7 fusion.260
  52.6 0.7 compare_bitcast_fusion.51
  63.8 0.7 fusion.260
  77.6 0.7 fusion.260
  80.1 0.7 compare_bitcast_fusion.51
  91.4 0.7 fusion.260
  105.1 1.4 copy.133
  106.5 0.8 rev.3
  107.4 1.7 broadcast_multiply_fusion
  109.1 1.3 copy.136
  110.4 1.4 convolution_convert_fusion.4
  112.3 20.5 %all_to_all.138 = bf16[12,96,2,128]{3,2,0,1:T(2,128)(2,1)S(1)} all-to-all(bf16[12,96,2,128]{3,2,0,1:T(2,128)(2,1)S(1)} %copy.139), channel_id=1, replica_groups=mesh['parts'=2,'space'=8,'chan'=2] {'space'}, dimensions={1} | all-to-all | bytes 1179648 | tf_op jit(solution)/shard_map/all_to_all | solution.py:109
  133.2 0.9 copy.142
  134.1 8.7 %all-gather.2.cloned.1.call-done = bf16[96,12,2,256]{3,0,2,1:T(8,128)(2,1)} async-done(((bf16[96,12,2,128]{3,0,2,1:T(8,128)(2,1)}), bf16[96,12,2,256]{3,0,2,1:T(8,128)(2,1)}) %all-gather.2.cloned.1.call-update) | async-done | bytes 1179664 | tf_op jit(solution)/shard_map/all_gather | solution.py:141
  142.9 1.7 fusion.182
  145.1 21.5 %all_to_all.139 = bf16[96,12,2,128]{3,2,1,0:T(2,128)(2,1)S(1)} all-to-all(bf16[96,12,2,128]{3,2,1,0:T(2,128)(2,1)S(1)} %copy.143), channel_id=1, replica_groups=mesh['parts'=2,'space'=8,'chan'=2] {'space'}, dimensions={0} | all-to-all | bytes 1179648 | tf_op jit(solution)/shard_map/all_to_all | solution.py:113
  167.5 1.0 copy.146
  168.5 5.4 %all-to-all-start.3 = ((bf16[96,24,128]{2,1,0:T(8,128)(2,1)}), bf16[96,24,128]{2,1,0:T(8,128)(2,1)}, u32[]{:S(2)}, u32[]{:S(2)}) async-start(bf16[96,24,128]{2,1,0:T(8,128)(2,1)} %copy.146), calls=%async_computation.3 | async-start | bytes 1179648 | tf_op jit(solution)/shard_map/all_to_all | solution.py:117
  174.1 13.5 %all-to-all-done.3 = bf16[96,24,128]{2,1,0:T(8,128)(2,1)} async-done(((bf16[96,24,128]{2,1,0:T(8,128)(2,1)}), bf16[96,24,128]{2,1,0:T(8,128)(2,1)}, u32[]{:S(2)}, u32[]{:S(2)}) %all-to-all-start.3) | async-done | bytes 589856 | tf_op jit(solution)/shard_map/all_to_all | solution.py:117
  187.5 1.1 copy.147
  188.7 4.2 %fusion.173 = (bf16[12,768,128]{2,1,0:T(8,128)(2,1)}, f32[768,12,128]{2,0,1:T(8,128)S(1)}) fusion(bf16[12,768,128]{2,1,0:T(8,128)(2,1)S(1)} %copy-done.1, bf16[12,192,128]{2,1,0:T(8,128)(2,1)S(1)} %bitcast.412, f32[768,192]{0,1:T(8,128)} %reshape.813, f32[192]{0:T(256)S(1)} %mul.926), kind=kOutput, calls=%fused_computation.325 | convolution fusion | flops 461537280 | bytes 10617600 | tf_op jit(solution)/shard_map/jnc,nk->jkc/dot_general | solution.py:153
  192.9 2.6 fusion.184
  196.0 23.3 %all_to_all.140 = bf16[12,192,128]{2,0,1:T(8,128)(2,1)S(1)} all-to-all(bf16[12,192,128]{2,0,1:T(8,128)(2,1)S(1)} %copy.149), channel_id=1, replica_groups=mesh['parts'=2,'space'=8,'chan'=2] {'space'}, dimensions={1} | all-to-all | bytes 1179648 | tf_op jit(solution)/shard_map/all_to_all | solution.py:105
  220.2 19.1 %all_to_all.141 = bf16[12,96,2,128]{3,2,0,1:T(2,128)(2,1)S(1)} all-to-all(bf16[12,96,2,128]{3,2,0,1:T(2,128)(2,1)S(1)} %copy.154), channel_id=1, replica_groups=mesh['parts'=2,'space'=8,'chan'=2] {'space'}, dimensions={1} | all-to-all | bytes 1179648 | tf_op jit(solution)/shard_map/all_to_all | solution.py:109
  239.7 0.8 copy-done.9
  240.6 1.5 fusion.177
  242.0 3.7 %copy.180 = bf16[96,12,2,256]{0,2,1,3:T(2,128)(2,1)S(1)} copy(bf16[96,12,2,256]{3,0,2,1:T(8,128)(2,1)} %fusion.177) | data formatting | bytes 2359296
  245.7 2.1 reshape.829
  247.8 8.2 %reduce-scatter.4.cloned.1.call-done = bf16[128,2304]{1,0:T(8,128)(2,1)} async-done(((bf16[256,2304]{1,0:T(8,128)(2,1)}), bf16[128,2304]{1,0:T(8,128)(2,1)}) %reduce-scatter.4.cloned.1.call-update) | async-done | bytes 589840
  256.0 3.3 %reshape.830 = bf16[128,12,2,96]{3,2,1,0:T(2,128)(2,1)S(1)} reshape(bf16[128,2304]{1,0:T(8,128)(2,1)} %reduce-scatter.4.cloned.1.call-done) | data formatting | bytes 1179648
  259.3 0.7 copy.181
  260.6 21.5 %all_to_all.142 = bf16[96,12,2,128]{3,2,1,0:T(2,128)(2,1)S(1)} all-to-all(bf16[96,12,2,128]{3,2,1,0:T(2,128)(2,1)S(1)} %copy.158), channel_id=1, replica_groups=mesh['parts'=2,'space'=8,'chan'=2] {'space'}, dimensions={0} | all-to-all | bytes 1179648 | tf_op jit(solution)/shard_map/all_to_all | solution.py:113
  283.1 1.0 copy.161
  284.1 4.7 %all-to-all-start.7 = ((bf16[96,24,128]{2,1,0:T(8,128)(2,1)}), bf16[96,24,128]{2,1,0:T(8,128)(2,1)S(1)}, u32[]{:S(2)}, u32[]{:S(2)}) async-start(bf16[96,24,128]{2,1,0:T(8,128)(2,1)} %copy.161), calls=%async_computation.7 | async-start | bytes 1179648 | tf_op jit(solution)/shard_map/all_to_all | solution.py:117
  289.4 2.8 fusion.176
  292.2 10.7 %all-to-all-done.7 = bf16[96,24,128]{2,1,0:T(8,128)(2,1)S(1)} async-done(((bf16[96,24,128]{2,1,0:T(8,128)(2,1)}), bf16[96,24,128]{2,1,0:T(8,128)(2,1)S(1)}, u32[]{:S(2)}, u32[]{:S(2)}) %all-to-all-start.7) | async-done | bytes 589856 | tf_op jit(solution)/shard_map/all_to_all | solution.py:117
  303.0 3.9 %fusion.164 = bf16[12,768,128]{2,1,0:T(8,128)(2,1)} fusion(bf16[12,768,128]{2,1,0:T(8,128)(2,1)} %param.7, bf16[768,192,1]{0,1,2:T(8,128)(2,1)S(1)} %reshape.826, bf16[12,192,128]{2,1,0:T(8,128)(2,1)S(1)} %bitcast.426), kind=kOutput, calls=%fused_computation.314 | convolution fusion | flops 456523776 | bytes 5603328 | tf_op jit(solution)/shard_map/jnc,kn->jkc/dot_general | solution.py:192
  (276 shorter events, 81.9 us)
Async XLA Ops:
  7.2 135.7 %copy-start = (bf16[12,256,128]{2,1,0:T(8,128)(2,1)S(1)}, bf16[12,256,128]{2,1,0:T(8,128)(2,1)}, u32[]{:S(2)}) copy-start(bf16[12,256,128]{2,1,0:T(8,128)(2,1)} %param.6) | copy-start | bytes 2359300
  7.2 5.7 %copy-start.1 = (bf16[12,768,128]{2,1,0:T(8,128)(2,1)S(1)}, bf16[12,768,128]{2,1,0:T(8,128)(2,1)}, u32[]{:S(2)}) copy-start(bf16[12,768,128]{2,1,0:T(8,128)(2,1)} %param.5) | copy-start | bytes 7077892
  8.4 0.7 copy-start.5
  8.4 0.8 copy-start.7
  15.8 93.3 %all-to-all-start = ((bf16[12,192,128]{2,0,1:T(8,128)(2,1)}), bf16[12,192,128]{2,0,1:T(8,128)(2,1)}, u32[]{:S(2)}, u32[]{:S(2)}) async-start(bf16[12,192,128]{2,0,1:T(8,128)(2,1)} %copy.134), calls=%async_computation | async-start | bytes 1572864 | tf_op jit(solution)/shard_map/all_to_all | solution.py:105
  22.1 120.8 %all-gather.2.cloned.1.call-start = ((), (), s32[]{:S(2)}) async-start(), calls=%async_computation.9 | async-start | bytes 1769472 | tf_op jit(solution)/shard_map/all_gather | solution.py:141
  144.6 22.5 %copy-start.2 = (f32[12,48,96]{2,1,0:T(8,128)S(1)}, f32[12,48,96]{2,1,0:T(8,128)}, u32[]{:S(2)}) copy-start(f32[12,48,96]{2,1,0:T(8,128)} %broadcast_multiply_fusion) | copy-start | bytes 663556
  168.5 19.1 %all-to-all-start.3 = ((bf16[96,24,128]{2,1,0:T(8,128)(2,1)}), bf16[96,24,128]{2,1,0:T(8,128)(2,1)}, u32[]{:S(2)}, u32[]{:S(2)}) async-start(bf16[96,24,128]{2,1,0:T(8,128)(2,1)} %copy.146), calls=%async_computation.3 | async-start | bytes 1179648 | tf_op jit(solution)/shard_map/all_to_all | solution.py:117
  173.9 82.2 %reduce-scatter.4.cloned.1.call-start = ((), (), s32[]{:S(2)}) async-start(), calls=%async_computation.10 | async-start | bytes 1769472
  188.7 4.2 %copy-start.4 = (f32[768,192]{0,1:T(8,128)S(1)}, f32[768,192]{0,1:T(8,128)}, u32[]{:S(2)}) copy-start(f32[768,192]{0,1:T(8,128)} %reshape.813) | copy-start | bytes 1769476
  188.7 4.2 %copy-start.11 = (bf16[12,768,128]{2,1,0:T(8,128)(2,1)S(1)}, bf16[12,768,128]{2,1,0:T(8,128)(2,1)}, u32[]{:S(2)}) copy-start(bf16[12,768,128]{2,1,0:T(8,128)(2,1)} %param.7) | copy-start | bytes 7077892
  195.5 23.8 %copy-start.3 = (f32[12,48,96]{2,1,0:T(8,128)S(1)}, f32[12,48,96]{2,1,0:T(8,128)}, u32[]{:S(2)}) copy-start(f32[12,48,96]{2,1,0:T(8,128)} %broadcast_multiply_fusion) | copy-start | bytes 663556
  239.7 0.8 copy-start.9
  282.7 6.2 %copy-start.6 = (f32[768,96,1]{0,1,2:T(8,128)S(1)}, f32[768,96,1]{0,1,2:T(8,128)}, u32[]{:S(2)}) copy-start(f32[768,96,1]{0,1,2:T(8,128)} %copy-done.5) | copy-start | bytes 884740
  282.7 6.2 %copy-start.8 = (f32[768,96,1]{0,1,2:T(8,128)S(1)}, f32[768,96,1]{0,1,2:T(8,128)}, u32[]{:S(2)}) copy-start(f32[768,96,1]{0,1,2:T(8,128)} %copy-done.7) | copy-start | bytes 884740
  283.1 6.3 %copy-start.10 = (bf16[8,12,12,2,128]{4,3,2,1,0:T(2,128)(2,1)S(1)}, bf16[8,12,12,2,128]{4,3,2,1,0:T(2,128)(2,1)}, u32[]{:S(2)}) copy-start(bf16[8,12,12,2,128]{4,3,2,1,0:T(2,128)(2,1)} %copy-done.9) | copy-start | bytes 1769476
  284.1 18.7 %all-to-all-start.7 = ((bf16[96,24,128]{2,1,0:T(8,128)(2,1)}), bf16[96,24,128]{2,1,0:T(8,128)(2,1)S(1)}, u32[]{:S(2)}, u32[]{:S(2)}) async-start(bf16[96,24,128]{2,1,0:T(8,128)(2,1)} %copy.161), calls=%async_computation.7 | async-start | bytes 1179648 | tf_op jit(solution)/shard_map/all_to_all | solution.py:117
Sparse Core Ops, SparseCore 0:
  134.3 8.5 all-gather.1
  248.0 8.0 reduce-scatter.3
where the time goes:
time: 318 us; the launch traced here: 314 us
  blocking collectives  106 us (33%)
  other arithmetic  75.6 us (24%)
  waiting for transfers between devices  41.1 us (13%)
  local copies, waits for them, and re-layouts  38.1 us (12%)
  matrix products  20.9 us (7%)
  starting transfers between devices  16.4 us (5%)
  between operations  14.4 us (5%)
    gt x96, other arithmetic, advance(): degree > order_col  60.9 us
    all_to_all x2, blocking collectives, from_degrees(): lax.all_to_all(values, 'space', split_axis=0, concat_axis=1, tiled=True)  43.1 us
    all_to_all x2, blocking collectives, into_degrees(): lax.all_to_all(values, 'space', split_axis=1, concat_axis=0, tiled=True)  39.6 us
    all_to_all x2, waiting for transfers between devices, into_latitudes(): lax.all_to_all(values, 'space', split_axis=0, concat_axis=1, tiled=True)  24.2 us
    all_to_all x1, blocking collectives, into_orders(): lax.all_to_all(values, 'space', split_axis=1, concat_axis=0, tiled=True)  23.3 us
    unnamed x28, local copies, waits for them, and re-layouts  11.4 us
    all_to_all x2, starting transfers between devices, into_latitudes(): lax.all_to_all(values, 'space', split_axis=0, concat_axis=1, tiled=True)  10.1 us
    while x90, other arithmetic  9.2 us
  transfers between devices with their start and end apart: 5, of which 4 were waited for; matrix products, arithmetic and copies ran while one was open for 28% of the time, Pallas kernels for 0%

commit v1 on v0

v1 whole, which is shorter than its diff:
```python
import functools
import math

import jax
import jax.numpy as jnp
import ml_dtypes
import numpy as np
from jax import lax
from jax.experimental import pallas as pl
from jax.experimental.pallas import tpu as pltpu
from jax.sharding import PartitionSpec as P

LIMIT = 2.0**40
SHRINK = 2.0 ** (-40)
LOGSTEP = 40.0 * math.log(2.0)
MESH = pl.DeviceIdType.MESH


def fourier_tables(longitudes, order_list):
    products = (np.asarray(order_list)[:, None] * np.arange(longitudes)[None, :]) % longitudes
    angle = 2.0 * math.pi / longitudes * products
    table = np.stack([np.cos(angle), -np.sin(angle)], axis=1)
    weights = np.where(np.asarray(order_list) == 0, 1.0, 2.0)[:, None, None]
    forward = table.reshape(-1, longitudes).astype(np.float32)
    inverse = (table * weights).reshape(-1, longitudes).astype(np.float32)
    return forward.astype(ml_dtypes.bfloat16), inverse.astype(ml_dtypes.bfloat16)


def latitude_rows(latitudes, longitudes, orders):
    half = latitudes // 2
    north = (np.arange(half) + 0.5) * (math.pi / latitudes)
    cosines = np.concatenate([np.cos(north), -np.cos(north)[::-1]])
    sines = np.concatenate([np.sin(north), np.sin(north)[::-1]])
    order = np.arange(orders)
    gammas = np.array([math.lgamma(m + 0.5) - math.lgamma(m + 1.0) for m in order])
    start = 0.5 * (np.log((2.0 * order + 1.0) / (4.0 * math.pi)) + gammas - 0.5 * math.log(math.pi))
    log_start = start[:, None] + order[:, None] * np.log(sines)[None, :]
    area = latitudes * longitudes
    rows = np.stack([cosines, math.pi**1.5 / math.sqrt(area) * sines])
    return (
        log_start.astype(np.float32),
        rows.astype(np.float32),
        math.sqrt(4.0 * math.pi / area),
    )


def legendre_into(log_start, rows, synthesis_scale, first_order, values, analysis, synthesis):
    held, degrees, latitudes = values.shape
    shape = (held, latitudes)
    order = (lax.broadcasted_iota(jnp.int32, shape, 0) + first_order).astype(jnp.float32)
    cosines = jnp.broadcast_to(rows[0:1, :], shape)
    start = log_start[...]

    def step(at, state):
        previous, before, rescales = state
        degree = at.astype(jnp.float32)
        lower_deg = degree - 1.0
        square = order * order
        upper = jnp.sqrt((4.0 * degree * degree - 1.0) / jnp.maximum(degree * degree - square, 1.0))
        lower = jnp.sqrt(
            jnp.maximum(lower_deg * lower_deg - square, 0.0)
            / jnp.maximum(4.0 * lower_deg * lower_deg - 1.0, 1.0)
        )
        newest = jnp.where(
            degree == order,
            1.0,
            jnp.where(degree > order, upper * (cosines * previous - lower * before), 0.0),
        )
        too_large = jnp.abs(newest) > LIMIT
        newest = jnp.where(too_large, newest * SHRINK, newest)
        previous = jnp.where(too_large, previous * SHRINK, previous)
        rescales = rescales + jnp.where(too_large, 1.0, 0.0)
        values[:, pl.ds(at, 1), :] = (newest * jnp.exp(start + rescales * LOGSTEP))[:, None, :]
        return newest, previous, rescales

    zero = jnp.zeros(shape, jnp.float32)
    lax.fori_loop(0, degrees, step, (zero, zero, zero))
    quadrature = rows[1:2, :]

    def finish(m, carry):
        analysis[m] = (values[m] * quadrature).astype(jnp.bfloat16)
        synthesis[m] = (values[m] * synthesis_scale).astype(jnp.bfloat16)
        return carry

    lax.fori_loop(0, held, finish, 0)


class Exchange:
    def __init__(self, n, held, spread, sparse):
        self.n, self.held, self.spread, self.sparse = n, held, spread, sparse

    def greet(self, chan):
        me = lax.axis_index("space")
        barrier = pltpu.get_barrier_semaphore()
        for k in range(1, self.n):
            pl.semaphore_signal(
                barrier, inc=1, device_id={"space": lax.rem(me + k, self.n)}, device_id_type=MESH
            )
        if chan:
            pl.semaphore_signal(
                barrier, inc=1, device_id={"chan": 1 - lax.axis_index("chan")}, device_id_type=MESH
            )
        pl.semaphore_wait(barrier, self.n - 1 + (1 if chan else 0))

    def source(self, x, d):
        return x.at[:, d] if self.spread else x.at[pl.ds(d * self.held, self.held)]

    def slot(self, y, s):
        return y.at[pl.ds(s * self.held, self.held)] if self.spread else y.at[:, s]

    def when(self, other, run):
        if self.sparse:
            pl.when(lax.axis_index("space") + other >= self.n - 1)(run)
        else:
            run()

    def copy(self, x, y, k, send_sem, recv_sem, sending):
        me = lax.axis_index("space")
        other = lax.rem(me + k, self.n) if sending else lax.rem(me + self.n - k, self.n)
        return other, pltpu.make_async_remote_copy(
            src_ref=self.source(x, other),
            dst_ref=self.slot(y, me if sending else other),
            send_sem=send_sem.at[k],
            recv_sem=recv_sem.at[k],
            device_id={"space": other},
            device_id_type=MESH,
        )


def send_all(ex, x, y, send_sem, recv_sem):
    for k in range(1, ex.n):
        other, copy = ex.copy(x, y, k, send_sem, recv_sem, True)
        ex.when(other, copy.start)


def wait_sends(ex, x, y, send_sem, recv_sem):
    for k in range(1, ex.n):
        other, copy = ex.copy(x, y, k, send_sem, recv_sem, True)
        ex.when(other, copy.wait_send)


def zero_fill(ex, targets, zero, zero_sem, start):
    me = lax.axis_index("space")
    for k in range(ex.n):
        other = lax.rem(me + ex.n - k, ex.n)

        @pl.when(me + other < ex.n - 1)
        def _():
            for i, y in enumerate(targets):
                copy = pltpu.make_async_copy(zero, ex.slot(y, other), zero_sem.at[i, k])
                copy.start() if start else copy.wait()


def plain_kernel(ex, legendre, *refs):
    if legendre is not None:
        x, log_start, rows, y, analysis, synthesis, values = refs[:7]
        send_sem, recv_sem, own_sem = refs[7:]
    elif ex.sparse:
        x, y, zero, zero_sem, send_sem, recv_sem, own_sem = refs
    else:
        x, y, send_sem, recv_sem, own_sem = refs
    me = lax.axis_index("space")
    ex.greet(False)
    send_all(ex, x, y, send_sem, recv_sem)
    own = pltpu.make_async_copy(ex.source(x, me), ex.slot(y, me), own_sem)
    ex.when(me, own.start)
    if ex.sparse:
        zero[...] = jnp.zeros_like(zero)
        zero_fill(ex, [y], zero, zero_sem, True)
    if legendre is not None:
        first_order = (ex.n - 1 - me) * ex.held
        legendre_into(log_start, rows, legendre, first_order, values, analysis, synthesis)
    ex.when(me, own.wait)
    for k in range(1, ex.n):
        other, copy = ex.copy(x, y, k, send_sem, recv_sem, False)
        ex.when(other, copy.wait_recv)
    wait_sends(ex, x, y, send_sem, recv_sem)
    if ex.sparse:
        zero_fill(ex, [y], zero, zero_sem, False)


def gather_kernel(ex, by_channel, x, y, zero, zero_sem, send_sem, recv_sem, own_sem, fsend, frecv):
    me = lax.axis_index("space")
    chan = lax.axis_index("chan")
    mine = y.at[chan] if by_channel else y.at[0]
    theirs = y.at[chan] if by_channel else y.at[1]
    coming = y.at[1 - chan] if by_channel else y.at[1]
    ex.greet(True)
    send_all(ex, x, mine, send_sem, recv_sem)

    def forward(k, other, source):
        return pltpu.make_async_remote_copy(
            src_ref=source,
            dst_ref=ex.slot(theirs, other),
            send_sem=fsend.at[k],
            recv_sem=frecv.at[k],
            device_id={"chan": 1 - chan},
            device_id_type=MESH,
        )

    own = pltpu.make_async_copy(ex.source(x, me), ex.slot(mine, me), own_sem)
    ex.when(me, own.start)
    ex.when(me, forward(0, me, ex.source(x, me)).start)
    zero[...] = jnp.zeros_like(zero)
    zero_fill(ex, [y.at[0], y.at[1]], zero, zero_sem, True)
    for k in range(1, ex.n):
        other, copy = ex.copy(x, mine, k, send_sem, recv_sem, False)

        def pass_on(copy=copy, k=k, other=other):
            copy.wait_recv()
            forward(k, other, ex.slot(mine, other)).start()

        ex.when(other, pass_on)
    ex.when(me, own.wait)
    for k in range(ex.n):
        other = lax.rem(me + ex.n - k, ex.n)

        def settle(k=k, other=other):
            copy = pltpu.make_async_remote_copy(
                src_ref=ex.slot(mine, other),
                dst_ref=ex.slot(coming, other),
                send_sem=fsend.at[k],
                recv_sem=frecv.at[k],
                device_id={"chan": 1 - chan},
                device_id_type=MESH,
            )
            copy.wait_recv()
            copy.wait_send()

        ex.when(other, settle)
    wait_sends(ex, x, mine, send_sem, recv_sem)
    zero_fill(ex, [y.at[0], y.at[1]], zero, zero_sem, False)


def any_spec():
    return pl.BlockSpec(memory_space=pl.ANY)


def vmem_spec():
    return pl.BlockSpec(memory_space=pltpu.VMEM)


def params(collective_id):
    return pltpu.CompilerParams(
        collective_id=collective_id, has_side_effects=True, vmem_limit_bytes=24 * 2**20
    )


def swap(x, n, spread, sparse, collective_id, legendre=None):
    if spread:
        held, _, rows, width = x.shape
        shape = (n * held, rows, width)
    else:
        total, rows, width = x.shape
        held = total // n
        shape = (held, n, rows, width)
    ex = Exchange(n, held, spread, sparse)
    sems = [
        pltpu.SemaphoreType.DMA((n,)),
        pltpu.SemaphoreType.DMA((n,)),
        pltpu.SemaphoreType.DMA,
    ]
    out = jax.ShapeDtypeStruct(shape, x.dtype)
    if legendre is not None:
        log_start, rows_in, scale = legendre
        orders, latitudes = log_start.shape
        table = jax.ShapeDtypeStruct((orders, n * held, latitudes), jnp.bfloat16)
        return pl.pallas_call(
            functools.partial(plain_kernel, ex, scale),
            out_shape=(out, table, table),
            in_specs=[any_spec(), vmem_spec(), vmem_spec()],
            out_specs=(any_spec(), vmem_spec(), vmem_spec()),
            scratch_shapes=[pltpu.VMEM((orders, n * held, latitudes), jnp.float32)] + sems,
            compiler_params=params(collective_id),
            name="exchange_and_legendre",
        )(x, log_start, rows_in)
    scratch = list(sems)
    if sparse:
        zeros = [pltpu.VMEM((held, rows, width), x.dtype), pltpu.SemaphoreType.DMA((1, n))]
        scratch = zeros + scratch
    return pl.pallas_call(
        functools.partial(plain_kernel, ex, None),
        out_shape=out,
        in_specs=[any_spec()],
        out_specs=any_spec(),
        scratch_shapes=scratch,
        compiler_params=params(collective_id),
        name="exchange",
    )(x)


def swap_gather(x, n, by_channel, collective_id):
    total, rows, width = x.shape
    held = total // n
    ex = Exchange(n, held, False, True)
    return pl.pallas_call(
        functools.partial(gather_kernel, ex, by_channel),
        out_shape=jax.ShapeDtypeStruct((2, held, n, rows, width), x.dtype),
        in_specs=[any_spec()],
        out_specs=any_spec(),
        scratch_shapes=[
            pltpu.VMEM((held, rows, width), x.dtype),
            pltpu.SemaphoreType.DMA((2, n)),
            pltpu.SemaphoreType.DMA((n,)),
            pltpu.SemaphoreType.DMA((n,)),
            pltpu.SemaphoreType.DMA,
            pltpu.SemaphoreType.DMA((n,)),
            pltpu.SemaphoreType.DMA((n,)),
        ],
        compiler_params=params(collective_id),
        name="exchange_and_gather",
    )(x)


def dot32(formula, left, right):
    return jnp.einsum(formula, left, right, preferred_element_type=jnp.float32)


def local(field, spectral_weight, cotangent):
    n = lax.axis_size("space")
    held, longitudes, half = field.shape
    degrees_held, channels, _ = spectral_weight.shape
    latitudes = held * n
    degrees = degrees_held * n
    orders_held = degrees_held
    rows = 2 * orders_held
    mix_scale = 1.0 / math.sqrt(channels)
    chan = lax.axis_index("chan")
    block = n - 1 - lax.axis_index("space")
    order_list = np.arange(degrees).reshape(n, orders_held)[::-1].reshape(-1)
    forward_np, inverse_np = fourier_tables(longitudes, order_list)
    forward, inverse = jnp.asarray(forward_np), jnp.asarray(inverse_np)
    log_np, rows_np, scale = latitude_rows(latitudes, longitudes, degrees)
    log_start = lax.dynamic_slice_in_dim(jnp.asarray(log_np), block * orders_held, orders_held, 0)

    weight_halves = spectral_weight.reshape(degrees_held, 2, half, half)
    weight_own = lax.dynamic_index_in_dim(weight_halves, chan, 1, keepdims=False)
    weight_give = lax.dynamic_index_in_dim(weight_halves, 1 - chan, 1, keepdims=False)
    weight_other = lax.ppermute(weight_give, "chan", [(0, 1), (1, 0)])

    fourier = dot32("jkc,nk->jnc", field, forward).astype(jnp.bfloat16)
    by_order, analysis, synthesis = swap(
        fourier.reshape(held, n, rows, half),
        n,
        True,
        False,
        0,
        (log_start, jnp.asarray(rows_np), scale),
    )

    def to_degrees(table, values):
        values = values.reshape(latitudes, orders_held, 2, half)
        out = dot32("mlj,jmrc->lmrc", table, values).astype(jnp.bfloat16)
        return out.reshape(degrees, rows, half)

    def to_latitudes(table, values):
        values = values.reshape(degrees, orders_held, 2, half)
        out = dot32("mlj,lmrc->jmrc", table, values).astype(jnp.bfloat16)
        return out.reshape(latitudes, rows, half)

    coeffs = swap_gather(to_degrees(analysis, by_order), n, True, 1)
    coeffs = coeffs.reshape(2, degrees_held, n * rows, half)
    mixed = (
        dot32("lqc,lco->lqo", coeffs[0], weight_halves[:, 0])
        + dot32("lqc,lco->lqo", coeffs[1], weight_halves[:, 1])
    ) * mix_scale
    mixed = mixed.astype(jnp.bfloat16).reshape(degrees_held, n, rows, half)
    mixed_orders = swap(mixed, n, True, True, 2)
    grid = swap(to_latitudes(synthesis, mixed_orders), n, False, False, 3)
    grid = grid.reshape(held, n * rows, half)
    response = dot32("jnc,nk->jkc", grid, inverse)
    normal_cdf = 0.5 * (1.0 + lax.erf(response * (1.0 / math.sqrt(2.0))))
    output = (field.astype(jnp.float32) + response * normal_cdf).astype(jnp.bfloat16)
    density = jnp.exp(-0.5 * response * response) * (1.0 / math.sqrt(2.0 * math.pi))
    response_grad = (cotangent.astype(jnp.float32) * (normal_cdf + response * density)).astype(
        jnp.bfloat16
    )
    grid_grad = dot32("jkc,nk->jnc", response_grad, inverse).astype(jnp.bfloat16)
    grad_by_order = swap(grid_grad.reshape(held, n, rows, half), n, True, False, 4)
    grads = swap_gather(to_degrees(synthesis, grad_by_order), n, False, 5)
    grads = grads.reshape(2, degrees_held, n * rows, half)
    coeff_grad = (
        dot32("lqo,lco->lqc", grads[0], weight_own) + dot32("lqo,lco->lqc", grads[1], weight_other)
    ) * mix_scale
    coeff_grad = coeff_grad.astype(jnp.bfloat16).reshape(degrees_held, n, rows, half)
    coeff_orders = swap(coeff_grad, n, True, True, 6)
    fourier_band = swap(to_latitudes(analysis, coeff_orders), n, False, False, 7)
    fourier_band = fourier_band.reshape(held, n * rows, half)
    weight_grad = (dot32("xlqc,lqo->lxco", coeffs, grads[0]) * mix_scale).astype(jnp.bfloat16)
    field_grad = (
        cotangent.astype(jnp.float32) + dot32("jnc,nk->jkc", fourier_band, forward)
    ).astype(jnp.bfloat16)
    return (output, field_grad, weight_grad.reshape(degrees_held, channels, half))


def solution(mesh):
    in_specs = (
        P(("parts", "space"), None, "chan"),
        P("space", None, "chan"),
        P(("parts", "space"), None, "chan"),
    )
    out_specs = (
        P(("parts", "space"), None, "chan"),
        P(("parts", "space"), None, "chan"),
        P(("parts", "space"), None, "chan"),
    )
    return jax.shard_map(local, mesh=mesh, in_specs=in_specs, out_specs=out_specs, check_vma=False)
```

time: 318 us -> 161 us (0.51)
  Pallas kernels: 0 us -> 121 us
  blocking collectives: 106 us -> 0 us
  other arithmetic: 75.6 us -> 0 us
  waiting for transfers between devices: 41.1 us -> 0.01 us
  local copies, waits for them, and re-layouts: 38.1 us -> 21.3 us
  starting transfers between devices: 16.4 us -> 0.01 us
  between operations: 14.4 us -> 0.89 us
  matrix products: 20.9 us -> 15.6 us
    pallas_call x0 -> x8, Pallas kernels: none -> 121 us  [the longest x5 75.9 us: swap(): pl.pallas_call(functools.partial(plain_kernel, ex, None), out_shape=out,...]
    all_to_all x5 -> x0, blocking collectives: 106 us -> none  [the longest x2 43.1 us: from_degrees(): lax.all_to_all(values, 'space', split_axis=0, concat_axis=1, tiled=True)]
    gt x96 -> x0, other arithmetic: 60.9 us -> none  [advance(): degree > order_col]
    all_to_all x3 -> x0, waiting for transfers between devices: 24.2 us -> none  [the longest x2 24.2 us: into_latitudes(): lax.all_to_all(values, 'space', split_axis=0, concat_axis=1, tiled=True)]
    all_to_all x3 -> x0, starting transfers between devices: 16.4 us -> none  [the longest x2 10.1 us: into_latitudes(): lax.all_to_all(values, 'space', split_axis=0, concat_axis=1, tiled=True)]
    while x90 -> x0, other arithmetic: 9.2 us -> none
    all_gather x1 -> x0, waiting for transfers between devices: 8.72 us -> none  [local(): all_channels = lax.all_gather(by_degree, 'chan', axis=3, tiled=True)]
    unnamed x3 -> x0, waiting for transfers between devices: 8.22 us -> none
  transfers between devices with their start and end apart: 5 -> 1, of which waited for: 4 -> 0; matrix products, arithmetic and copies ran while one was open for 28% -> 19% of each run, Pallas kernels for 0% -> 57%
where the time goes in v1:
time: 161 us; the launch traced here: 159 us
  Pallas kernels  121 us (75%)
  local copies, waits for them, and re-layouts  21.3 us (13%)
  matrix products  15.6 us (10%)
    pallas_call x5, Pallas kernels, swap(): pl.pallas_call(functools.partial(plain_kernel, ex, None), out_shape=out,...  75.9 us
    pallas_call x2, Pallas kernels, swap_gather(): pl.pallas_call(functools.partial(gather_kernel, ex, by_channel), out_shap...  28.4 us
    pallas_call x1, Pallas kernels, swap(): pl.pallas_call(functools.partial(plain_kernel, ex, scale), out_shape=(out...  16.9 us
    dot_general x13, matrix products, dot32(): return jnp.einsum(formula, left, right, preferred_element_type=jnp.float32)  15.6 us
    unnamed x24, local copies, waits for them, and re-layouts  15.5 us
  transfers between devices with their start and end apart: 1, of which 0 were waited for; matrix products, arithmetic and copies ran while one was open for 19% of the time, Pallas kernels for 57%

profile of v1, /device:TPU:8, one launch (start us, length us, event | category | flops | bytes accessed | tf_op | source)
XLA Modules:
  0.0 159.1 jit_solution(193891943431228558)
XLA Ops:
  0.6 1.8 %dynamic-slice_bitcast_fusion = bf16[12,128,128]{2,1,0:T(8,128)(2,1)} fusion(bf16[12,2,128,128]{3,2,1,0:T(8,128)(2,1)} %bitcast.126, s32[]{:T(128)S(6)} %select_n.12), kind=kLoop, calls=%fused_computation.44 | loop fusion | bytes 786436 | tf_op jit(solution)/shard_map/jit(dynamic_index_in_dim)/squeeze | solution.py:338
  2.4 0.0 collective-permute-start
  2.4 4.4 %copy.26 = bf16[12,768,128]{1,2,0:T(8,128)(2,1)} copy(bf16[12,768,128]{2,1,0:T(8,128)(2,1)} %param.7) | data formatting | bytes 4718592 | tf_op args[0]
  6.8 0.0 copy-done.1
  6.8 0.0 copy-done.7
  6.8 0.7 convolution_convert_fusion.4
  7.5 0.7 constant_dynamic-slice_fusion.refs_1_
  8.2 0.0 copy-done
  8.2 16.9 %exchange_and_legendre.1 = (bf16[96,24,128]{2,1,0:T(8,128)(2,1)S(1)}, bf16[12,96,96]{2,1,0:T(8,128)(2,1)S(1)}, bf16[12,96,96]{2,1,0:T(8,128)(2,1)S(1)}) custom-call(bf16[12,8,24,128]{3,2,1,0:T(8,128)(2,1)S(1)} %bitcast.113, f32[12,96]{1,0:T(8,128)S(1)} %constant_dynamic-slice_fusion.refs_1_, f32[2,96]{1,0:T(2,128)S(1)} %copy-done), custom_call_target="tpu_custom_call" | custom-call | tf_op jit(solution)/shard_map/exchange_and_legendre/pallas_call | solution.py:268
  25.2 0.3 fusion.22
  25.5 0.5 copy.28
  26.0 0.0 copy-start.4
  26.0 15.2 %exchange_and_gather.2 = bf16[2,12,8,24,128]{4,3,2,1,0:T(8,128)(2,1)S(1)} custom-call(bf16[96,24,128]{2,1,0:T(8,128)(2,1)S(1)} %bitcast.114), custom_call_target="tpu_custom_call" | custom-call | tf_op jit(solution)/shard_map/exchange_and_gather/pallas_call | solution.py:296
  41.2 0.2 fusion.42
  41.4 0.0 copy-done.4
  41.4 0.3 fusion.29
  41.7 0.3 fusion.15
  42.0 13.4 %exchange.5 = bf16[96,24,128]{2,1,0:T(8,128)(2,1)S(1)} custom-call(bf16[12,8,24,128]{3,2,1,0:T(8,128)(2,1)S(1)} %bitcast.120), custom_call_target="tpu_custom_call" | custom-call | tf_op jit(solution)/shard_map/exchange/pallas_call | solution.py:281
  55.4 0.4 fusion.20
  55.8 0.5 copy.33
  56.3 16.6 %exchange.6 = bf16[12,8,24,128]{3,2,1,0:T(8,128)(2,1)S(1)} custom-call(bf16[96,24,128]{2,1,0:T(8,128)(2,1)S(1)} %bitcast.116), custom_call_target="tpu_custom_call" | custom-call | tf_op jit(solution)/shard_map/exchange/pallas_call | solution.py:281
  72.9 0.0 copy-start.9
  72.9 4.3 %copy.34 = bf16[12,768,128]{1,2,0:T(8,128)(2,1)} copy(bf16[12,768,128]{2,1,0:T(8,128)(2,1)} %param.9) | data formatting | bytes 4718592 | tf_op args[2]
  77.2 0.0 copy-done.9
  77.2 4.8 %fusion.10 = (bf16[12,768,128]{1,2,0:T(8,128)(2,1)}, f32[12,128,768]{2,1,0:T(8,128)S(1)}) fusion(bf16[12,768,128]{1,2,0:T(8,128)(2,1)} %copy.26, bf16[12,192,128]{2,1,0:T(8,128)(2,1)S(1)} %bitcast.112, bf16[192,768,1]{1,0,2:T(8,128)(2,1)S(1)} %copy-done.9), kind=kOutput, calls=%fused_computation.15 | convolution fusion | flops 461242368 | bytes 10321920 | tf_op jit(solution)/shard_map/jnc,nk->jkc/dot_general | solution.py:316
  82.1 0.0 copy-done.2
  82.1 2.9 %fusion.17 = bf16[12,128,192]{1,2,0:T(8,128)(2,1)S(1)} fusion(bf16[192,768,1]{1,0,2:T(8,128)(2,1)S(1)} %copy-done.9, bf16[12,768,128]{1,2,0:T(8,128)(2,1)S(1)} %copy-done.2, f32[12,128,768]{2,1,0:T(8,128)S(1)} %get-tuple-element.20), kind=kOutput, calls=%fused_computation.24 | convolution fusion | flops 466255872 | bytes 7962624 | tf_op jit(solution)/shard_map/jkc,nk->jnc/dot_general | solution.py:316
  85.0 16.1 %exchange.7 = bf16[96,24,128]{2,1,0:T(8,128)(2,1)S(1)} custom-call(bf16[12,8,24,128]{3,2,1,0:T(8,128)(2,1)S(1)} %bitcast.124), custom_call_target="tpu_custom_call" | custom-call | tf_op jit(solution)/shard_map/exchange/pallas_call | solution.py:281
  101.1 0.3 fusion.23
  101.5 0.5 copy.37
  101.9 13.2 %exchange_and_gather.3 = bf16[2,12,8,24,128]{4,3,2,1,0:T(8,128)(2,1)S(1)} custom-call(bf16[96,24,128]{2,1,0:T(8,128)(2,1)S(1)} %bitcast.115), custom_call_target="tpu_custom_call" | custom-call | tf_op jit(solution)/shard_map/exchange_and_gather/pallas_call | solution.py:296
  115.2 1.2 fusion.41
  116.4 1.4 fusion.30
  117.8 4.3 %copy.42 = bf16[12,768,128]{2,1,0:T(8,128)(2,1)} copy(bf16[12,768,128]{1,2,0:T(8,128)(2,1)} %get-tuple-element.19) | data formatting | bytes 4718592
  122.2 0.0 copy-done.5
  122.2 1.5 multiply_convert_fusion
  123.7 0.0 collective-permute-done
  123.7 0.0 copy-done.6
  123.7 1.4 fusion.16
  125.1 0.0 copy-start.8
  125.1 13.8 %exchange.8 = bf16[96,24,128]{2,1,0:T(8,128)(2,1)S(1)} custom-call(bf16[12,8,24,128]{3,2,1,0:T(8,128)(2,1)S(1)} %bitcast.118), custom_call_target="tpu_custom_call" | custom-call | tf_op jit(solution)/shard_map/exchange/pallas_call | solution.py:281
  139.0 0.4 fusion.21
  139.3 0.5 copy.40
  139.8 16.0 %exchange.9 = bf16[12,8,24,128]{3,2,1,0:T(8,128)(2,1)S(1)} custom-call(bf16[96,24,128]{2,1,0:T(8,128)(2,1)S(1)} %bitcast.117), custom_call_target="tpu_custom_call" | custom-call | tf_op jit(solution)/shard_map/exchange/pallas_call | solution.py:281
  155.8 0.0 copy-done.3
  155.8 0.0 copy-done.8
  155.8 0.8 fusion.1
  156.7 2.4 %copy.43 = bf16[12,768,128]{2,1,0:T(8,128)(2,1)} copy(bf16[12,768,128]{1,2,0:T(8,128)(2,1)S(1)} %fusion.1) | data formatting | bytes 4718592
  (7 shorter events, 0.0 us)
Async XLA Ops:
  2.4 121.3 %collective-permute-start = (bf16[12,128,128]{2,1,0:T(8,128)(2,1)}, bf16[12,128,128]{2,1,0:T(8,128)(2,1)}, u32[]{:S(2)}, u32[]{:S(2)}) collective-permute-start(bf16[12,128,128]{2,1,0:T(8,128)(2,1)} %dynamic-slice_bitcast_fusion), channel_id=1, source_target_pairs={{0,1},{1,0},{2,3},{3,2},{4,5},{5,4},{6,7},{7,6},{8,9},{9,8},{10,11... | collective-permute-start | bytes 1179656 | tf_op jit(solution)/shard_map/ppermute | solution.py:339
  2.4 4.4 %copy-start.1 = (bf16[12,768,128]{2,1,0:T(8,128)(2,1)S(1)}, bf16[12,768,128]{2,1,0:T(8,128)(2,1)}, u32[]{:S(2)}) copy-start(bf16[12,768,128]{2,1,0:T(8,128)(2,1)} %param.7) | copy-start | bytes 7077892
  2.4 4.4 %copy-start.7 = (bf16[192,768,1]{1,0,2:T(8,128)(2,1)S(1)}, bf16[192,768,1]{1,0,2:T(8,128)(2,1)}, u32[]{:S(2)}) copy-start(bf16[192,768,1]{1,0,2:T(8,128)(2,1)} %constant.55) | copy-start | bytes 884740
  6.8 1.4 copy-start
  26.0 15.4 %copy-start.4 = (bf16[12,256,128]{2,1,0:T(8,128)(2,1)S(1)}, bf16[12,256,128]{2,1,0:T(8,128)(2,1)}, u32[]{:S(2)}) copy-start(bf16[12,256,128]{2,1,0:T(8,128)(2,1)} %param.8) | copy-start | bytes 2359300
  72.9 4.3 %copy-start.9 = (bf16[192,768,1]{1,0,2:T(8,128)(2,1)S(1)}, bf16[192,768,1]{1,0,2:T(8,128)(2,1)}, u32[]{:S(2)}) copy-start(bf16[192,768,1]{1,0,2:T(8,128)(2,1)} %constant.56) | copy-start | bytes 884740
  77.2 4.9 %copy-start.2 = (bf16[12,768,128]{1,2,0:T(8,128)(2,1)S(1)}, bf16[12,768,128]{1,2,0:T(8,128)(2,1)}, u32[]{:S(2)}) copy-start(bf16[12,768,128]{1,2,0:T(8,128)(2,1)} %copy.34) | copy-start | bytes 7077892
  117.8 4.3 %copy-start.5 = (bf16[1,12,8,24,128]{4,3,2,1,0:T(8,128)(2,1)S(1)}, bf16[1,12,8,24,128]{4,3,2,1,0:T(8,128)(2,1)}, u32[]{:S(2)}) copy-start(bf16[1,12,8,24,128]{4,3,2,1,0:T(8,128)(2,1)} %get-tuple-element.16) | copy-start | bytes 1769476
  122.2 1.5 copy-start.6
  125.1 30.7 %copy-start.3 = (bf16[12,768,128]{1,2,0:T(8,128)(2,1)S(1)}, bf16[12,768,128]{1,2,0:T(8,128)(2,1)}, u32[]{:S(2)}) copy-start(bf16[12,768,128]{1,2,0:T(8,128)(2,1)} %copy.34) | copy-start | bytes 7077892
  125.1 30.7 %copy-start.8 = (bf16[192,768,1]{1,0,2:T(8,128)(2,1)S(1)}, bf16[192,768,1]{1,0,2:T(8,128)(2,1)}, u32[]{:S(2)}) copy-start(bf16[192,768,1]{1,0,2:T(8,128)(2,1)} %constant.55) | copy-start | bytes 884740

commit v2 on v1

--- a/solution.py
+++ b/solution.py
@@ -312,6 +312,388 @@
     )(x)
 
 
+def flat(block):
+    rows = block.shape[0] * block.shape[1]
+    return block.astype(jnp.float32).reshape(rows, block.shape[2]).astype(block.dtype)
+
+
+def unflat(values, n):
+    return values.reshape(n, values.shape[0] // n, values.shape[1]).astype(jnp.bfloat16)
+
+
+def mm(left, right):
+    return jnp.dot(left, right, preferred_element_type=jnp.float32)
+
+
+CHUNK = 4
+
+
+class Chunked:
+    def __init__(self, n, held):
+        self.n, self.held = n, held
+        self.chunks = held // CHUNK
+
+    def band(self, f, c, d):
+        return f.at[pl.ds(c * CHUNK, CHUNK), d]
+
+    def lats(self, y, c, s):
+        return y.at[pl.ds(s * self.held + c * CHUNK, CHUNK)]
+
+    def copy(self, x, y, c, k, send_sem, recv_sem, sending, outward):
+        me = lax.axis_index("space")
+        other = lax.rem(me + k, self.n) if sending else lax.rem(me + self.n - k, self.n)
+        here = me if sending else other
+        if outward:
+            src, dst = self.band(x, c, other), self.lats(y, c, here)
+        else:
+            src, dst = self.lats(x, c, other), self.band(y, c, here)
+        return pltpu.make_async_remote_copy(
+            src_ref=src,
+            dst_ref=dst,
+            send_sem=send_sem.at[c, k],
+            recv_sem=recv_sem.at[c, k],
+            device_id={"space": other},
+            device_id_type=MESH,
+        )
+
+    def own(self, x, y, c, sem, outward):
+        me = lax.axis_index("space")
+        if outward:
+            return pltpu.make_async_copy(self.band(x, c, me), self.lats(y, c, me), sem.at[c])
+        return pltpu.make_async_copy(self.lats(x, c, me), self.band(y, c, me), sem.at[c])
+
+
+def fourier_kernel(
+    ex,
+    synthesis_scale,
+    field,
+    weight,
+    forward,
+    log_start,
+    rows,
+    y,
+    analysis,
+    synthesis,
+    weights,
+    values,
+    held_field,
+    bands,
+    load_sem,
+    send_sem,
+    recv_sem,
+    own_sem,
+    weight_sem,
+):
+    n, ch = ex.n, Chunked(ex.n, ex.held)
+    me = lax.axis_index("space")
+    chan = lax.axis_index("chan")
+    half = weight.shape[2]
+    loads = [
+        pltpu.make_async_copy(
+            field.at[pl.ds(c * CHUNK, CHUNK)], held_field.at[pl.ds(c * CHUNK, CHUNK)], load_sem.at[c]
+        )
+        for c in range(ch.chunks)
+    ]
+    for load in loads:
+        load.start()
+    ex.greet(True)
+    keep = pltpu.make_async_copy(
+        weight.at[:, pl.ds(pl.multiple_of(chan * half, half), half)], weights.at[0], weight_sem.at[0]
+    )
+    give = pltpu.make_async_remote_copy(
+        src_ref=weight.at[:, pl.ds(pl.multiple_of((1 - chan) * half, half), half)],
+        dst_ref=weights.at[1],
+        send_sem=weight_sem.at[1],
+        recv_sem=weight_sem.at[2],
+        device_id={"chan": 1 - chan},
+        device_id_type=MESH,
+    )
+    for c in range(ch.chunks):
+        loads[c].wait()
+
+        def pair(i, carry, c=c):
+            j = c * CHUNK + 2 * i
+            wide = jnp.concatenate([held_field[j], held_field[j + 1]], axis=1)
+            out = mm(forward[...], wide)
+            bands[j] = unflat(out[:, :half], n)
+            bands[j + 1] = unflat(out[:, half:], n)
+            return carry
+
+        lax.fori_loop(0, CHUNK // 2, pair, 0)
+        for k in range(1, n):
+            ch.copy(bands, y, c, k, send_sem, recv_sem, True, True).start()
+        ch.own(bands, y, c, own_sem, True).start()
+    keep.start()
+    give.start()
+    first_order = (n - 1 - me) * ex.held
+    legendre_into(log_start, rows, synthesis_scale, first_order, values, analysis, synthesis)
+    for c in range(ch.chunks):
+        ch.own(bands, y, c, own_sem, True).wait()
+        for k in range(1, n):
+            ch.copy(bands, y, c, k, send_sem, recv_sem, False, True).wait_recv()
+            ch.copy(bands, y, c, k, send_sem, recv_sem, True, True).wait_send()
+    keep.wait()
+    give.wait()
+
+
+def fourier_exchange(field, weight, forward, n, rows, log_start, rows_in, scale, collective_id):
+    held, longitudes, half = field.shape
+    orders, latitudes = log_start.shape
+    degrees = weight.shape[0]
+    ex = Exchange(n, held, True, False)
+    chunks = held // CHUNK
+    table = jax.ShapeDtypeStruct((orders, degrees * n, latitudes), jnp.bfloat16)
+    return pl.pallas_call(
+        functools.partial(fourier_kernel, ex, scale),
+        out_shape=(
+            jax.ShapeDtypeStruct((n * held, rows, half), field.dtype),
+            table,
+            table,
+            jax.ShapeDtypeStruct((2, degrees, half, half), field.dtype),
+        ),
+        in_specs=[any_spec(), any_spec(), vmem_spec(), vmem_spec(), vmem_spec()],
+        out_specs=(any_spec(), vmem_spec(), vmem_spec(), any_spec()),
+        scratch_shapes=[
+            pltpu.VMEM((orders, degrees * n, latitudes), jnp.float32),
+            pltpu.VMEM((held, longitudes, half), field.dtype),
+            pltpu.VMEM((held, n, rows, half), field.dtype),
+            pltpu.SemaphoreType.DMA((chunks,)),
+            pltpu.SemaphoreType.DMA((chunks, n)),
+            pltpu.SemaphoreType.DMA((chunks, n)),
+            pltpu.SemaphoreType.DMA((chunks,)),
+            pltpu.SemaphoreType.DMA((3,)),
+        ],
+        compiler_params=params(collective_id),
+        name="fourier_exchange",
+    )(field, weight, forward, log_start, rows_in)
+
+
+TILE = 128
+
+
+def response_kernel(
+    ex,
+    grid,
+    field,
+    cotangent,
+    inverse_t,
+    inverse,
+    output,
+    y,
+    held_field,
+    held_cot,
+    arrived,
+    slopes,
+    bands,
+    load_sem,
+    in_send,
+    in_recv,
+    in_own,
+    out_send,
+    out_recv,
+    out_own,
+    store_sem,
+):
+    n, ch = ex.n, Chunked(ex.n, ex.held)
+    half = field.shape[2]
+    tiles = field.shape[1] // TILE
+
+    def part(ref, c):
+        return ref.at[pl.ds(c * CHUNK, CHUNK)]
+
+    def loads(c):
+        return (
+            pltpu.make_async_copy(part(field, c), part(held_field, c), load_sem.at[0, c]),
+            pltpu.make_async_copy(part(cotangent, c), part(held_cot, c), load_sem.at[1, c]),
+        )
+
+    def store(c):
+        return pltpu.make_async_copy(part(held_field, c), part(output, c), store_sem.at[c])
+
+    for c in range(ch.chunks):
+        for load in loads(c):
+            load.start()
+    ex.greet(False)
+    for c in range(ch.chunks):
+        for k in range(1, n):
+            ch.copy(grid, arrived, c, k, in_send, in_recv, True, False).start()
+        ch.own(grid, arrived, c, in_own, False).start()
+    for c in range(ch.chunks):
+        for load in loads(c):
+            load.wait()
+        ch.own(grid, arrived, c, in_own, False).wait()
+        for k in range(1, n):
+            ch.copy(grid, arrived, c, k, in_send, in_recv, False, False).wait_recv()
+
+        def pair(i, carry, c=c):
+            j = c * CHUNK + 2 * i
+            wide = jnp.concatenate([flat(arrived[j]), flat(arrived[j + 1])], axis=1)
+
+            def tile(t, inner):
+                at = pl.ds(pl.multiple_of(t * TILE, TILE), TILE)
+                response = mm(inverse_t[at, :], wide)
+                cdf = 0.5 * (1.0 + lax.erf(response * (1.0 / math.sqrt(2.0))))
+                density = jnp.exp(-0.5 * response * response) * (1.0 / math.sqrt(2.0 * math.pi))
+                gain = response * cdf
+                slope = cdf + response * density
+                for side in range(2):
+                    lanes = slice(side * half, (side + 1) * half)
+                    base = held_field[j + side, at, :].astype(jnp.float32)
+                    held_field[j + side, at, :] = (base + gain[:, lanes]).astype(jnp.bfloat16)
+                    cot = held_cot[j + side, at, :].astype(jnp.float32)
+                    slopes[at, lanes] = (cot * slope[:, lanes]).astype(jnp.bfloat16)
+                return inner
+
+            lax.fori_loop(0, tiles, tile, 0)
+            out = mm(inverse[...], slopes[...])
+            bands[j] = unflat(out[:, :half], n)
+            bands[j + 1] = unflat(out[:, half:], n)
+            return carry
+
+        lax.fori_loop(0, CHUNK // 2, pair, 0)
+        for k in range(1, n):
+            ch.copy(bands, y, c, k, out_send, out_recv, True, True).start()
+        ch.own(bands, y, c, out_own, True).start()
+        store(c).start()
+    for c in range(ch.chunks):
+        ch.own(bands, y, c, out_own, True).wait()
+        store(c).wait()
+        for k in range(1, n):
+            ch.copy(bands, y, c, k, out_send, out_recv, False, True).wait_recv()
+            ch.copy(bands, y, c, k, out_send, out_recv, True, True).wait_send()
+            ch.copy(grid, arrived, c, k, in_send, in_recv, True, False).wait_send()
+
+
+def response_exchange(grid, field, cotangent, inverse_t, inverse, n, collective_id):
+    held, longitudes, half = field.shape
+    rows = grid.shape[1]
+    chunks = held // CHUNK
+    ex = Exchange(n, held, True, False)
+    return pl.pallas_call(
+        functools.partial(response_kernel, ex),
+        out_shape=(
+            jax.ShapeDtypeStruct(field.shape, field.dtype),
+            jax.ShapeDtypeStruct((n * held, rows, half), field.dtype),
+        ),
+        in_specs=[any_spec()] * 3 + [vmem_spec()] * 2,
+        out_specs=(any_spec(), any_spec()),
+        scratch_shapes=[
+            pltpu.VMEM((held, longitudes, half), field.dtype),
+            pltpu.VMEM((held, longitudes, half), field.dtype),
+            pltpu.VMEM((held, n, rows, half), field.dtype),
+            pltpu.VMEM((longitudes, 2 * half), field.dtype),
+            pltpu.VMEM((held, n, rows, half), field.dtype),
+            pltpu.SemaphoreType.DMA((2, chunks)),
+            pltpu.SemaphoreType.DMA((chunks, n)),
+            pltpu.SemaphoreType.DMA((chunks, n)),
+            pltpu.SemaphoreType.DMA((chunks,)),
+            pltpu.SemaphoreType.DMA((chunks, n)),
+            pltpu.SemaphoreType.DMA((chunks, n)),
+            pltpu.SemaphoreType.DMA((chunks,)),
+            pltpu.SemaphoreType.DMA((chunks,)),
+        ],
+        compiler_params=params(collective_id),
+        name="response_exchange",
+    )(grid, field, cotangent, inverse_t, inverse)
+
+
+def field_grad_kernel(band, cotangent, forward_t, out):
+    half = band.shape[-1]
+    for i in range(0, band.shape[0], 2):
+        wide = jnp.concatenate([flat(band[i]), flat(band[i + 1])], axis=1)
+        total = mm(forward_t[...], wide)
+        for side in range(2):
+            part = total[:, side * half : (side + 1) * half]
+            out[i + side] = (cotangent[i + side].astype(jnp.float32) + part).astype(out.dtype)
+
+
+def final_field_grad(band, cotangent, forward_t):
+    held, n, rows, half = band.shape
+    longitudes = cotangent.shape[1]
+    lat = pl.BlockSpec((2, longitudes, half), lambda i: (i, 0, 0))
+    return pl.pallas_call(
+        field_grad_kernel,
+        grid=(held // 2,),
+        out_shape=jax.ShapeDtypeStruct(cotangent.shape, cotangent.dtype),
+        in_specs=[
+            pl.BlockSpec((2, n, rows, half), lambda i: (i, 0, 0, 0)),
+            lat,
+            pl.BlockSpec(forward_t.shape, lambda i: (0, 0)),
+        ],
+        out_specs=lat,
+        compiler_params=pltpu.CompilerParams(vmem_limit_bytes=24 * 2**20),
+        name="field_grad",
+    )(band, cotangent, forward_t)
+
+
+def mix_back_kernel(
+    ex, scale, coeffs, grads, weights, y, weight_grad, mixed, zero, zero_sem, send_sem, recv_sem, own_sem
+):
+    n = ex.n
+    me = lax.axis_index("space")
+    half = weights.shape[-1]
+    ex.greet(False)
+    turned = (((1,), (1,)), ((), ()))
+
+    def degree(at, carry):
+        total = lax.dot_general(
+            flat(grads[0, at]), weights[0, at], turned, preferred_element_type=jnp.float32
+        ) + lax.dot_general(
+            flat(grads[1, at]), weights[1, at], turned, preferred_element_type=jnp.float32
+        )
+        mixed[at] = unflat(total * scale, n)
+        return carry
+
+    lax.fori_loop(0, ex.held, degree, 0)
+    send_all(ex, mixed, y, send_sem, recv_sem)
+    own = pltpu.make_async_copy(ex.source(mixed, me), ex.slot(y, me), own_sem)
+    ex.when(me, own.start)
+    zero[...] = jnp.zeros_like(zero)
+    zero_fill(ex, [y], zero, zero_sem, True)
+    summed = (((0,), (0,)), ((), ()))
+
+    def products(at, carry):
+        grad = flat(grads[0, at])
+        for side in range(2):
+            part = lax.dot_general(
+                flat(coeffs[side, at]), grad, summed, preferred_element_type=jnp.float32
+            )
+            weight_grad[at, pl.ds(side * half, half), :] = (part * scale).astype(jnp.bfloat16)
+        return carry
+
+    lax.fori_loop(0, ex.held, products, 0)
+    ex.when(me, own.wait)
+    for k in range(1, n):
+        other, copy = ex.copy(mixed, y, k, send_sem, recv_sem, False)
+        ex.when(other, copy.wait_recv)
+    wait_sends(ex, mixed, y, send_sem, recv_sem)
+    zero_fill(ex, [y], zero, zero_sem, False)
+
+
+def mix_back(coeffs, grads, weights, scale, collective_id):
+    _, held, n, rows, half = coeffs.shape
+    ex = Exchange(n, held, True, True)
+    return pl.pallas_call(
+        functools.partial(mix_back_kernel, ex, scale),
+        out_shape=(
+            jax.ShapeDtypeStruct((n * held, rows, half), coeffs.dtype),
+            jax.ShapeDtypeStruct((held, 2 * half, half), coeffs.dtype),
+        ),
+        in_specs=[vmem_spec()] * 3,
+        out_specs=(any_spec(), vmem_spec()),
+        scratch_shapes=[
+            pltpu.VMEM((held, n, rows, half), coeffs.dtype),
+            pltpu.VMEM((held, rows, half), coeffs.dtype),
+            pltpu.SemaphoreType.DMA((1, n)),
+            pltpu.SemaphoreType.DMA((n,)),
+            pltpu.SemaphoreType.DMA((n,)),
+            pltpu.SemaphoreType.DMA,
+        ],
+        compiler_params=params(collective_id),
+        name="mix_back",
+    )(coeffs, grads, weights)
+
+
 def dot32(formula, left, right):
     return jnp.einsum(formula, left, right, preferred_element_type=jnp.float32)
 
@@ -334,18 +716,8 @@
     log_start = lax.dynamic_slice_in_dim(jnp.asarray(log_np), block * orders_held, orders_held, 0)
 
     weight_halves = spectral_weight.reshape(degrees_held, 2, half, half)
-    weight_own = lax.dynamic_index_in_dim(weight_halves, chan, 1, keepdims=False)
-    weight_give = lax.dynamic_index_in_dim(weight_halves, 1 - chan, 1, keepdims=False)
-    weight_other = lax.ppermute(weight_give, "chan", [(0, 1), (1, 0)])
-
-    fourier = dot32("jkc,nk->jnc", field, forward).astype(jnp.bfloat16)
-    by_order, analysis, synthesis = swap(
-        fourier.reshape(held, n, rows, half),
-        n,
-        True,
-        False,
-        0,
-        (log_start, jnp.asarray(rows_np), scale),
+    by_order, analysis, synthesis, weights = fourier_exchange(
+        field, spectral_weight, forward, n, rows, log_start, jnp.asarray(rows_np), scale, 0
     )
 
     def to_degrees(table, values):
@@ -358,39 +730,30 @@
         out = dot32("mlj,lmrc->jmrc", table, values).astype(jnp.bfloat16)
         return out.reshape(latitudes, rows, half)
 
-    coeffs = swap_gather(to_degrees(analysis, by_order), n, True, 1)
-    coeffs = coeffs.reshape(2, degrees_held, n * rows, half)
+    blocks = swap_gather(to_degrees(analysis, by_order), n, True, 1)
+    coeffs = blocks.reshape(2, degrees_held, n * rows, half)
     mixed = (
         dot32("lqc,lco->lqo", coeffs[0], weight_halves[:, 0])
         + dot32("lqc,lco->lqo", coeffs[1], weight_halves[:, 1])
     ) * mix_scale
     mixed = mixed.astype(jnp.bfloat16).reshape(degrees_held, n, rows, half)
     mixed_orders = swap(mixed, n, True, True, 2)
-    grid = swap(to_latitudes(synthesis, mixed_orders), n, False, False, 3)
-    grid = grid.reshape(held, n * rows, half)
-    response = dot32("jnc,nk->jkc", grid, inverse)
-    normal_cdf = 0.5 * (1.0 + lax.erf(response * (1.0 / math.sqrt(2.0))))
-    output = (field.astype(jnp.float32) + response * normal_cdf).astype(jnp.bfloat16)
-    density = jnp.exp(-0.5 * response * response) * (1.0 / math.sqrt(2.0 * math.pi))
-    response_grad = (cotangent.astype(jnp.float32) * (normal_cdf + response * density)).astype(
-        jnp.bfloat16
-    )
-    grid_grad = dot32("jkc,nk->jnc", response_grad, inverse).astype(jnp.bfloat16)
-    grad_by_order = swap(grid_grad.reshape(held, n, rows, half), n, True, False, 4)
+    output, grad_by_order = response_exchange(
+        to_latitudes(synthesis, mixed_orders),
+        field,
+        cotangent,
+        jnp.asarray(np.ascontiguousarray(inverse_np.T)),
+        inverse,
+        n,
+        3,
+    )
     grads = swap_gather(to_degrees(synthesis, grad_by_order), n, False, 5)
-    grads = grads.reshape(2, degrees_held, n * rows, half)
-    coeff_grad = (
-        dot32("lqo,lco->lqc", grads[0], weight_own) + dot32("lqo,lco->lqc", grads[1], weight_other)
-    ) * mix_scale
-    coeff_grad = coeff_grad.astype(jnp.bfloat16).reshape(degrees_held, n, rows, half)
-    coeff_orders = swap(coeff_grad, n, True, True, 6)
+    coeff_orders, weight_grad = mix_back(blocks, grads, weights, mix_scale, 6)
     fourier_band = swap(to_latitudes(analysis, coeff_orders), n, False, False, 7)
-    fourier_band = fourier_band.reshape(held, n * rows, half)
-    weight_grad = (dot32("xlqc,lqo->lxco", coeffs, grads[0]) * mix_scale).astype(jnp.bfloat16)
-    field_grad = (
-        cotangent.astype(jnp.float32) + dot32("jnc,nk->jkc", fourier_band, forward)
-    ).astype(jnp.bfloat16)
-    return (output, field_grad, weight_grad.reshape(degrees_held, channels, half))
+    field_grad = final_field_grad(
+        fourier_band, cotangent, jnp.asarray(np.ascontiguousarray(forward_np.T))
+    )
+    return (output, field_grad, weight_grad)
 
 
 def solution(mesh):

time: 161 us -> 140 us (0.87)
  matrix products: 15.6 us -> 1.99 us
  local copies, waits for them, and re-layouts: 21.3 us -> 10.3 us
  Pallas kernels: 121 us -> 125 us
    pallas_call x1 -> x4, Pallas kernels: 16.9 us -> 69 us  [the longest x1 32.2 us: response_exchange(): pl.pallas_call(functools.partial(response_kernel, ex), out_shape=(jax.Sha...]
    pallas_call x5 -> x2, Pallas kernels: 75.9 us -> 29.5 us  [swap(): pl.pallas_call(functools.partial(plain_kernel, ex, None), out_shape=out,...]
    dot_general x13 -> x6, matrix products: 15.6 us -> 1.99 us  [dot32(): return jnp.einsum(formula, left, right, preferred_element_type=jnp.float32)]
    unnamed x24 -> x20, local copies, waits for them, and re-layouts: 15.5 us -> 7.54 us
    squeeze x1 -> x0, local copies, waits for them, and re-layouts: 1.78 us -> none  [local(): lax.dynamic_index_in_dim(weight_halves, 1 - chan, 1, keepdims=False)]
    pallas_call x2, Pallas kernels: 28.4 us -> 26.7 us  [swap_gather(): pl.pallas_call(functools.partial(gather_kernel, ex, by_channel), out_shap...]
  transfers between devices with their start and end apart: 1 -> 0, of which waited for: 0 -> 0; matrix products, arithmetic and copies ran while one was open for 19% -> 0% of each run, Pallas kernels for 57% -> 0%
where the time goes in v2:
time: 140 us; the launch traced here: 138 us
  Pallas kernels  125 us (89%)
  local copies, waits for them, and re-layouts  10.3 us (7%)
  matrix products  1.99 us (1%)
    pallas_call x1, Pallas kernels, response_exchange(): pl.pallas_call(functools.partial(response_kernel, ex), out_shape=(jax.Sha...  32.2 us
    pallas_call x2, Pallas kernels, swap(): pl.pallas_call(functools.partial(plain_kernel, ex, None), out_shape=out,...  29.5 us
    pallas_call x2, Pallas kernels, swap_gather(): pl.pallas_call(functools.partial(gather_kernel, ex, by_channel), out_shap...  26.7 us
    pallas_call x1, Pallas kernels, fourier_exchange(): pl.pallas_call(functools.partial(fourier_kernel, ex, scale), out_shape=(j...  18.2 us
    pallas_call x1, Pallas kernels, mix_back(): pl.pallas_call(functools.partial(mix_back_kernel, ex, scale), out_shape=(...  15.2 us
    unnamed x20, local copies, waits for them, and re-layouts  7.54 us
    pallas_call x1, Pallas kernels, final_field_grad(): pl.pallas_call(field_grad_kernel, grid=(held // 2,), out_shape=jax.ShapeD...  3.33 us

profile of v2, /device:TPU:8, one launch (start us, length us, event | category | flops | bytes accessed | tf_op | source)
XLA Modules:
  0.0 138.3 jit_solution(34251247366174324)
XLA Ops:
  0.6 0.7 constant_dynamic-slice_fusion.log_start
  1.4 0.0 copy-start
  1.4 1.7 %copy-done = bf16[12,768,128]{2,1,0:T(8,128)(2,1)S(1)} copy-done((bf16[12,768,128]{2,1,0:T(8,128)(2,1)S(1)}, bf16[12,768,128]{2,1,0:T(8,128)(2,1)}, u32[]{:S(2)}) %copy-start) | copy-done | bytes 2359320
  3.0 0.0 copy-start.3
  3.0 1.1 copy-done.3
  4.2 0.0 copy-start.7
  4.2 1.0 copy-done.7
  5.1 0.0 copy-start.8
  5.1 0.7 copy-done.8
  5.8 18.2 %fourier_exchange.1 = (bf16[96,24,128]{2,1,0:T(8,128)(2,1)S(1)}, bf16[12,96,96]{2,1,0:T(8,128)(2,1)S(1)}, bf16[12,96,96]{2,1,0:T(8,128)(2,1)S(1)}, bf16[2,12,128,128]{3,2,1,0:T(8,128)(2,1)S(1)}) custom-call(bf16[12,768,128]{2,1,0:T(8,128)(2,1)S(1)} %copy-done, bf16[12,256,128]{2,1,0:T(8,128)(2,1)S(1)} %copy-done.3, bf16[192,768]{1,0:T(8,128)(2,1)S(1)} %copy-done.7, ...), custom_call_target="tpu_custom_call" | custom-call | tf_op jit(solution)/shard_map/fourier_exchange/pallas_call | solution.py:446
  24.0 0.3 fusion.4
  24.3 0.5 copy.23
  24.8 13.8 %exchange_and_gather.2.coeffs = bf16[2,12,8,24,128]{4,3,2,1,0:T(8,128)(2,1)S(1)} custom-call(bf16[96,24,128]{2,1,0:T(8,128)(2,1)S(1)} %bitcast.55), custom_call_target="tpu_custom_call" | custom-call | tf_op jit(solution)/shard_map/exchange_and_gather/pallas_call | solution.py:296
  38.6 0.2 fusion.15
  38.8 0.3 fusion.10
  39.1 0.0 copy-start.2
  39.1 0.3 fusion.1
  39.5 0.0 copy-start.5
  39.5 13.4 %exchange.2 = bf16[96,24,128]{2,1,0:T(8,128)(2,1)S(1)} custom-call(bf16[12,8,24,128]{3,2,1,0:T(8,128)(2,1)S(1)} %bitcast.58), custom_call_target="tpu_custom_call" | custom-call | tf_op jit(solution)/shard_map/exchange/pallas_call | solution.py:281
  52.9 0.0 copy-start.1
  52.9 0.0 copy-start.6
  52.9 0.4 fusion.2
  53.3 0.5 copy.28
  53.8 0.0 copy-done.2
  53.8 0.0 copy-done.5
  53.8 0.8 copy-done.1
  54.6 0.0 copy-done.6
  54.6 32.2 %response_exchange.1 = (bf16[12,768,128]{2,1,0:T(8,128)(2,1)S(1)}, bf16[96,24,128]{2,1,0:T(8,128)(2,1)S(1)}) custom-call(bf16[96,24,128]{2,1,0:T(8,128)(2,1)S(1)} %bitcast.54, bf16[12,768,128]{2,1,0:T(8,128)(2,1)S(1)} %copy-done.1, bf16[12,768,128]{2,1,0:T(8,128)(2,1)S(1)} %copy-done.2, bf16[768,192]{1,0:T(8,128)(2,1)S(1)} %copy-done.5, ...), custom_call_target="tpu_custom_call" | custom-call | tf_op jit(solution)/shard_map/response_exchange/pallas_call | solution.py:572
  86.8 0.3 fusion.5
  87.1 0.5 copy.30
  87.6 12.9 %exchange_and_gather.3.grads = bf16[2,12,8,24,128]{4,3,2,1,0:T(8,128)(2,1)S(1)} custom-call(bf16[96,24,128]{2,1,0:T(8,128)(2,1)S(1)} %bitcast.56), custom_call_target="tpu_custom_call" | custom-call | tf_op jit(solution)/shard_map/exchange_and_gather/pallas_call | solution.py:296
  100.5 15.2 %mix_back.1 = (bf16[96,24,128]{2,1,0:T(8,128)(2,1)S(1)}, bf16[12,256,128]{2,1,0:T(8,128)(2,1)S(1)}) custom-call(bf16[2,12,8,24,128]{4,3,2,1,0:T(8,128)(2,1)S(1)} %exchange_and_gather.2.coeffs, bf16[2,12,8,24,128]{4,3,2,1,0:T(8,128)(2,1)S(1)} %exchange_and_gather.3.grads, bf16[2,12,128,128]{3,2,1,0:T(8,128)(2,1)S(1)} %get-tuple-element.16.weights), custom_call_target="tpu_custom_call" | custom-call | tf_op jit(solution)/shard_map/mix_back/pallas_call | solution.py:676
  115.7 0.4 fusion.3
  116.1 0.0 copy-start.4
  116.1 0.5 copy.33
  116.6 16.1 %exchange.3.band = bf16[12,8,24,128]{3,2,1,0:T(8,128)(2,1)S(1)} custom-call(bf16[96,24,128]{2,1,0:T(8,128)(2,1)S(1)} %bitcast.57), custom_call_target="tpu_custom_call" | custom-call | tf_op jit(solution)/shard_map/exchange/pallas_call | solution.py:281
  132.7 0.0 copy-done.4
  132.7 3.3 %field_grad.1 = bf16[12,768,128]{2,1,0:T(8,128)(2,1)} custom-call(bf16[12,8,24,128]{3,2,1,0:T(8,128)(2,1)S(1)} %exchange.3.band, bf16[12,768,128]{2,1,0:T(8,128)(2,1)S(1)} %copy-done.2, bf16[768,192]{1,0:T(8,128)(2,1)S(1)} %copy-done.4), custom_call_target="tpu_custom_call" | custom-call | tf_op jit(solution)/shard_map/field_grad/pallas_call | solution.py:614
  136.0 1.4 %copy.54 = bf16[12,768,128]{2,1,0:T(8,128)(2,1)} copy(bf16[12,768,128]{2,1,0:T(8,128)(2,1)S(1)} %get-tuple-element.24) | data formatting | bytes 4718592
  137.4 0.9 copy.55
Async XLA Ops:
  1.4 1.7 %copy-start = (bf16[12,768,128]{2,1,0:T(8,128)(2,1)S(1)}, bf16[12,768,128]{2,1,0:T(8,128)(2,1)}, u32[]{:S(2)}) copy-start(bf16[12,768,128]{2,1,0:T(8,128)(2,1)} %field.3) | copy-start | bytes 7077892
  3.0 1.1 copy-start.3
  4.2 1.0 copy-start.7
  5.1 0.7 copy-start.8
  39.1 14.7 %copy-start.2 = (bf16[12,768,128]{2,1,0:T(8,128)(2,1)S(1)}, bf16[12,768,128]{2,1,0:T(8,128)(2,1)}, u32[]{:S(2)}) copy-start(bf16[12,768,128]{2,1,0:T(8,128)(2,1)} %cotangent.3) | copy-start | bytes 7077892
  39.5 14.3 %copy-start.5 = (bf16[768,192]{1,0:T(8,128)(2,1)S(1)}, bf16[768,192]{1,0:T(8,128)(2,1)}, u32[]{:S(2)}) copy-start(bf16[768,192]{1,0:T(8,128)(2,1)} %constant.32.clone.inverse_t) | copy-start | bytes 884740
  52.9 1.7 %copy-start.1 = (bf16[12,768,128]{2,1,0:T(8,128)(2,1)S(1)}, bf16[12,768,128]{2,1,0:T(8,128)(2,1)}, u32[]{:S(2)}) copy-start(bf16[12,768,128]{2,1,0:T(8,128)(2,1)} %field.3) | copy-start | bytes 7077892
  52.9 1.7 %copy-start.6 = (bf16[192,768]{1,0:T(8,128)(2,1)S(1)}, bf16[192,768]{1,0:T(8,128)(2,1)}, u32[]{:S(2)}) copy-start(bf16[192,768]{1,0:T(8,128)(2,1)} %constant.29.clone.inverse) | copy-start | bytes 884740
  116.1 16.6 %copy-start.4 = (bf16[768,192]{1,0:T(8,128)(2,1)S(1)}, bf16[768,192]{1,0:T(8,128)(2,1)}, u32[]{:S(2)}) copy-start(bf16[768,192]{1,0:T(8,128)(2,1)} %constant.33.clone.forward_t) | copy-start | bytes 884740

commit v3 on v2

--- a/solution.py
+++ b/solution.py
@@ -179,61 +179,12 @@
         zero_fill(ex, [y], zero, zero_sem, False)
 
 
-def gather_kernel(ex, by_channel, x, y, zero, zero_sem, send_sem, recv_sem, own_sem, fsend, frecv):
-    me = lax.axis_index("space")
-    chan = lax.axis_index("chan")
-    mine = y.at[chan] if by_channel else y.at[0]
-    theirs = y.at[chan] if by_channel else y.at[1]
-    coming = y.at[1 - chan] if by_channel else y.at[1]
-    ex.greet(True)
-    send_all(ex, x, mine, send_sem, recv_sem)
-
-    def forward(k, other, source):
-        return pltpu.make_async_remote_copy(
-            src_ref=source,
-            dst_ref=ex.slot(theirs, other),
-            send_sem=fsend.at[k],
-            recv_sem=frecv.at[k],
-            device_id={"chan": 1 - chan},
-            device_id_type=MESH,
-        )
-
-    own = pltpu.make_async_copy(ex.source(x, me), ex.slot(mine, me), own_sem)
-    ex.when(me, own.start)
-    ex.when(me, forward(0, me, ex.source(x, me)).start)
-    zero[...] = jnp.zeros_like(zero)
-    zero_fill(ex, [y.at[0], y.at[1]], zero, zero_sem, True)
-    for k in range(1, ex.n):
-        other, copy = ex.copy(x, mine, k, send_sem, recv_sem, False)
-
-        def pass_on(copy=copy, k=k, other=other):
-            copy.wait_recv()
-            forward(k, other, ex.slot(mine, other)).start()
-
-        ex.when(other, pass_on)
-    ex.when(me, own.wait)
-    for k in range(ex.n):
-        other = lax.rem(me + ex.n - k, ex.n)
-
-        def settle(k=k, other=other):
-            copy = pltpu.make_async_remote_copy(
-                src_ref=ex.slot(mine, other),
-                dst_ref=ex.slot(coming, other),
-                send_sem=fsend.at[k],
-                recv_sem=frecv.at[k],
-                device_id={"chan": 1 - chan},
-                device_id_type=MESH,
-            )
-            copy.wait_recv()
-            copy.wait_send()
-
-        ex.when(other, settle)
-    wait_sends(ex, x, mine, send_sem, recv_sem)
-    zero_fill(ex, [y.at[0], y.at[1]], zero, zero_sem, False)
-
-
 def any_spec():
     return pl.BlockSpec(memory_space=pl.ANY)
+
+
+def hbm_spec():
+    return pl.BlockSpec(memory_space=pltpu.HBM)
 
 
 def vmem_spec():
@@ -289,29 +240,6 @@
     )(x)
 
 
-def swap_gather(x, n, by_channel, collective_id):
-    total, rows, width = x.shape
-    held = total // n
-    ex = Exchange(n, held, False, True)
-    return pl.pallas_call(
-        functools.partial(gather_kernel, ex, by_channel),
-        out_shape=jax.ShapeDtypeStruct((2, held, n, rows, width), x.dtype),
-        in_specs=[any_spec()],
-        out_specs=any_spec(),
-        scratch_shapes=[
-            pltpu.VMEM((held, rows, width), x.dtype),
-            pltpu.SemaphoreType.DMA((2, n)),
-            pltpu.SemaphoreType.DMA((n,)),
-            pltpu.SemaphoreType.DMA((n,)),
-            pltpu.SemaphoreType.DMA,
-            pltpu.SemaphoreType.DMA((n,)),
-            pltpu.SemaphoreType.DMA((n,)),
-        ],
-        compiler_params=params(collective_id),
-        name="exchange_and_gather",
-    )(x)
-
-
 def flat(block):
     rows = block.shape[0] * block.shape[1]
     return block.astype(jnp.float32).reshape(rows, block.shape[2]).astype(block.dtype)
@@ -425,7 +353,7 @@
         ch.own(bands, y, c, own_sem, True).start()
     keep.start()
     give.start()
-    first_order = (n - 1 - me) * ex.held
+    first_order = (n - 1 - order_block(me)) * analysis.shape[0]
     legendre_into(log_start, rows, synthesis_scale, first_order, values, analysis, synthesis)
     for c in range(ch.chunks):
         ch.own(bands, y, c, own_sem, True).wait()
@@ -451,7 +379,7 @@
             table,
             jax.ShapeDtypeStruct((2, degrees, half, half), field.dtype),
         ),
-        in_specs=[any_spec(), any_spec(), vmem_spec(), vmem_spec(), vmem_spec()],
+        in_specs=[hbm_spec(), hbm_spec(), vmem_spec(), vmem_spec(), vmem_spec()],
         out_specs=(any_spec(), vmem_spec(), vmem_spec(), any_spec()),
         scratch_shapes=[
             pltpu.VMEM((orders, degrees * n, latitudes), jnp.float32),
@@ -575,7 +503,7 @@
             jax.ShapeDtypeStruct(field.shape, field.dtype),
             jax.ShapeDtypeStruct((n * held, rows, half), field.dtype),
         ),
-        in_specs=[any_spec()] * 3 + [vmem_spec()] * 2,
+        in_specs=[any_spec(), hbm_spec(), hbm_spec()] + [vmem_spec()] * 2,
         out_specs=(any_spec(), any_spec()),
         scratch_shapes=[
             pltpu.VMEM((held, longitudes, half), field.dtype),
@@ -626,72 +554,218 @@
     )(band, cotangent, forward_t)
 
 
-def mix_back_kernel(
-    ex, scale, coeffs, grads, weights, y, weight_grad, mixed, zero, zero_sem, send_sem, recv_sem, own_sem
-):
-    n = ex.n
+def order_block(s):
+    return s + ((s // 2) % 2) * (1 - 2 * (s % 2))
+
+
+def holds(n, orders_at, degrees_at):
+    return order_block(orders_at) + degrees_at >= n - 1
+
+
+def degree_kernel(n, backward, scale, *refs):
+    if backward:
+        x, weights, coeffs, y, weight_grad, blocks = refs[:6]
+    else:
+        x, weights, y, blocks = refs[:4]
+    mixed, zero, zero_sem, send1, recv1, own1, fsend, frecv, send2, recv2, own2 = refs[-11:]
     me = lax.axis_index("space")
-    half = weights.shape[-1]
-    ex.greet(False)
-    turned = (((1,), (1,)), ((), ()))
-
-    def degree(at, carry):
-        total = lax.dot_general(
-            flat(grads[0, at]), weights[0, at], turned, preferred_element_type=jnp.float32
-        ) + lax.dot_general(
-            flat(grads[1, at]), weights[1, at], turned, preferred_element_type=jnp.float32
+    chan = lax.axis_index("chan")
+    held, half = blocks.shape[1], blocks.shape[-1]
+    mine = pl.ds(pl.multiple_of(chan * half, half), half)
+    theirs = pl.ds(pl.multiple_of((1 - chan) * half, half), half)
+    Exchange(n, held, False, True).greet(True)
+
+    def ahead(k):
+        return lax.rem(me + k, n)
+
+    def behind(k):
+        return lax.rem(me + n - k, n)
+
+    def rows_of(ref, d):
+        return ref.at[pl.ds(d * held, held)]
+
+    def coming(k, sending):
+        return pltpu.make_async_remote_copy(
+            src_ref=rows_of(x, ahead(k)),
+            dst_ref=blocks.at[0, :, me if sending else behind(k)],
+            send_sem=send1.at[k],
+            recv_sem=recv1.at[k],
+            device_id={"space": ahead(k) if sending else behind(k)},
+            device_id_type=MESH,
         )
-        mixed[at] = unflat(total * scale, n)
+
+    def across(k):
+        return pltpu.make_async_remote_copy(
+            src_ref=blocks.at[0, :, behind(k)],
+            dst_ref=blocks.at[1, :, behind(k)],
+            send_sem=fsend.at[k],
+            recv_sem=frecv.at[k],
+            device_id={"chan": 1 - chan},
+            device_id_type=MESH,
+        )
+
+    def going(k, sending):
+        return pltpu.make_async_remote_copy(
+            src_ref=mixed.at[:, behind(k)],
+            dst_ref=rows_of(y, me if sending else ahead(k)),
+            send_sem=send2.at[k],
+            recv_sem=recv2.at[k],
+            device_id={"space": behind(k) if sending else ahead(k)},
+            device_id_type=MESH,
+        )
+
+    def start_coming(k, carry):
+        pl.when(holds(n, me, ahead(k)))(lambda: coming(k, True).start())
         return carry
 
-    lax.fori_loop(0, ex.held, degree, 0)
-    send_all(ex, mixed, y, send_sem, recv_sem)
-    own = pltpu.make_async_copy(ex.source(mixed, me), ex.slot(y, me), own_sem)
-    ex.when(me, own.start)
+    lax.fori_loop(1, n, start_coming, 0)
+    own_in = pltpu.make_async_copy(rows_of(x, me), blocks.at[0, :, me], own1)
+    own_out = pltpu.make_async_copy(mixed.at[:, me], rows_of(y, me), own2)
     zero[...] = jnp.zeros_like(zero)
-    zero_fill(ex, [y], zero, zero_sem, True)
-    summed = (((0,), (0,)), ((), ()))
-
-    def products(at, carry):
-        grad = flat(grads[0, at])
-        for side in range(2):
-            part = lax.dot_general(
-                flat(coeffs[side, at]), grad, summed, preferred_element_type=jnp.float32
-            )
-            weight_grad[at, pl.ds(side * half, half), :] = (part * scale).astype(jnp.bfloat16)
+
+    def zeros_of(k):
+        return pltpu.make_async_copy(zero, rows_of(y, ahead(k)), zero_sem.at[k])
+
+    def fill(k, carry):
+        other = behind(k)
+
+        @pl.when(jnp.logical_not(holds(n, other, me)))
+        def _():
+            for side in range(2):
+                for at in range(held):
+                    blocks[side, at, other] = jnp.zeros(blocks.shape[3:], blocks.dtype)
+
+        pl.when(jnp.logical_not(holds(n, me, ahead(k))))(lambda: zeros_of(k).start())
         return carry
 
-    lax.fori_loop(0, ex.held, products, 0)
-    ex.when(me, own.wait)
-    for k in range(1, n):
-        other, copy = ex.copy(mixed, y, k, send_sem, recv_sem, False)
-        ex.when(other, copy.wait_recv)
-    wait_sends(ex, mixed, y, send_sem, recv_sem)
-    zero_fill(ex, [y], zero, zero_sem, False)
-
-
-def mix_back(coeffs, grads, weights, scale, collective_id):
-    _, held, n, rows, half = coeffs.shape
-    ex = Exchange(n, held, True, True)
+    def mix(other):
+        for at in range(held):
+            wide = jnp.concatenate([blocks[0, at, other], blocks[1, at, other]], axis=1)
+            if backward:
+                weight = jnp.concatenate([weights[0, at], weights[1, at]], axis=1)
+                total = lax.dot_general(
+                    wide, weight, (((1,), (1,)), ((), ())), preferred_element_type=jnp.float32
+                )
+            else:
+                weight = jnp.concatenate([weights[at, mine, :], weights[at, theirs, :]], axis=0)
+                total = mm(wide, weight)
+            mixed[at, other] = (total * scale).astype(mixed.dtype)
+
+    has_own = holds(n, me, me)
+
+    @pl.when(has_own)
+    def _():
+        own_in.start()
+        own_in.wait()
+        across(0).start()
+
+    lax.fori_loop(0, n, fill, 0)
+
+    def settle(k):
+        across(k).wait_recv()
+        mix(behind(k))
+        going(k, True).start()
+
+    def turn(k, carry):
+        @pl.when(holds(n, behind(k), me))
+        def _():
+            coming(k, False).wait_recv()
+            across(k).start()
+
+        @pl.when(jnp.logical_and(k > 1, holds(n, behind(k - 1), me)))
+        def _():
+            settle(k - 1)
+
+        return carry
+
+    lax.fori_loop(1, n, turn, 0)
+    pl.when(holds(n, behind(n - 1), me))(lambda: settle(n - 1))
+
+    @pl.when(has_own)
+    def _():
+        across(0).wait_recv()
+        mix(me)
+        own_out.start()
+
+    if backward:
+
+        def products(at, carry):
+            grad = flat(blocks[0, at])
+            for side, lines in ((0, mine), (1, theirs)):
+                part = lax.dot_general(
+                    flat(coeffs[side, at]),
+                    grad,
+                    (((0,), (0,)), ((), ())),
+                    preferred_element_type=jnp.float32,
+                )
+                weight_grad[at, lines, :] = (part * scale).astype(weight_grad.dtype)
+            return carry
+
+        lax.fori_loop(0, held, products, 0)
+
+    @pl.when(has_own)
+    def _():
+        own_out.wait()
+        across(0).wait_send()
+
+    def finish(k, carry):
+        @pl.when(holds(n, behind(k), me))
+        def _():
+            across(k).wait_send()
+            going(k, True).wait_send()
+
+        @pl.when(holds(n, me, ahead(k)))
+        def _():
+            coming(k, True).wait_send()
+            going(k, False).wait_recv()
+
+        return carry
+
+    lax.fori_loop(1, n, finish, 0)
+
+    def filled(k, carry):
+        pl.when(jnp.logical_not(holds(n, me, ahead(k))))(lambda: zeros_of(k).wait())
+        return carry
+
+    lax.fori_loop(0, n, filled, 0)
+
+
+def degree_exchange(x, weights, n, scale, collective_id, coeffs=None):
+    total, rows, half = x.shape
+    held = total // n
+    backward = coeffs is not None
+    block = jax.ShapeDtypeStruct((2, held, n, rows, half), x.dtype)
+    shapes = [jax.ShapeDtypeStruct(x.shape, x.dtype)]
+    specs = [any_spec(), vmem_spec()]
+    scratch = []
+    if backward:
+        shapes.append(jax.ShapeDtypeStruct((held, 2 * half, half), x.dtype))
+        scratch.append(pltpu.VMEM(block.shape, x.dtype))
+    else:
+        shapes.append(block)
+    dma = pltpu.SemaphoreType.DMA
     return pl.pallas_call(
-        functools.partial(mix_back_kernel, ex, scale),
-        out_shape=(
-            jax.ShapeDtypeStruct((n * held, rows, half), coeffs.dtype),
-            jax.ShapeDtypeStruct((held, 2 * half, half), coeffs.dtype),
-        ),
-        in_specs=[vmem_spec()] * 3,
-        out_specs=(any_spec(), vmem_spec()),
-        scratch_shapes=[
-            pltpu.VMEM((held, n, rows, half), coeffs.dtype),
-            pltpu.VMEM((held, rows, half), coeffs.dtype),
-            pltpu.SemaphoreType.DMA((1, n)),
-            pltpu.SemaphoreType.DMA((n,)),
-            pltpu.SemaphoreType.DMA((n,)),
-            pltpu.SemaphoreType.DMA,
+        functools.partial(degree_kernel, n, backward, scale),
+        out_shape=tuple(shapes),
+        in_specs=[any_spec()] + [vmem_spec()] * (2 if backward else 1),
+        out_specs=tuple(specs),
+        scratch_shapes=scratch
+        + [
+            pltpu.VMEM((held, n, rows, half), x.dtype),
+            pltpu.VMEM((held, rows, half), x.dtype),
+            dma((n,)),
+            dma((n,)),
+            dma((n,)),
+            dma,
+            dma((n,)),
+            dma((n,)),
+            dma((n,)),
+            dma((n,)),
+            dma,
         ],
         compiler_params=params(collective_id),
-        name="mix_back",
-    )(coeffs, grads, weights)
+        name="degree_exchange",
+    )(*([x, weights] + ([coeffs] if backward else [])))
 
 
 def dot32(formula, left, right):
@@ -708,14 +782,14 @@
     rows = 2 * orders_held
     mix_scale = 1.0 / math.sqrt(channels)
     chan = lax.axis_index("chan")
-    block = n - 1 - lax.axis_index("space")
-    order_list = np.arange(degrees).reshape(n, orders_held)[::-1].reshape(-1)
+    block = n - 1 - order_block(lax.axis_index("space"))
+    held_blocks = [n - 1 - order_block(s) for s in range(n)]
+    order_list = np.arange(degrees).reshape(n, orders_held)[held_blocks].reshape(-1)
     forward_np, inverse_np = fourier_tables(longitudes, order_list)
     forward, inverse = jnp.asarray(forward_np), jnp.asarray(inverse_np)
     log_np, rows_np, scale = latitude_rows(latitudes, longitudes, degrees)
     log_start = lax.dynamic_slice_in_dim(jnp.asarray(log_np), block * orders_held, orders_held, 0)
 
-    weight_halves = spectral_weight.reshape(degrees_held, 2, half, half)
     by_order, analysis, synthesis, weights = fourier_exchange(
         field, spectral_weight, forward, n, rows, log_start, jnp.asarray(rows_np), scale, 0
     )
@@ -730,14 +804,9 @@
         out = dot32("mlj,lmrc->jmrc", table, values).astype(jnp.bfloat16)
         return out.reshape(latitudes, rows, half)
 
-    blocks = swap_gather(to_degrees(analysis, by_order), n, True, 1)
-    coeffs = blocks.reshape(2, degrees_held, n * rows, half)
-    mixed = (
-        dot32("lqc,lco->lqo", coeffs[0], weight_halves[:, 0])
-        + dot32("lqc,lco->lqo", coeffs[1], weight_halves[:, 1])
-    ) * mix_scale
-    mixed = mixed.astype(jnp.bfloat16).reshape(degrees_held, n, rows, half)
-    mixed_orders = swap(mixed, n, True, True, 2)
+    mixed_orders, coeffs = degree_exchange(
+        to_degrees(analysis, by_order), spectral_weight, n, mix_scale, 1
+    )
     output, grad_by_order = response_exchange(
         to_latitudes(synthesis, mixed_orders),
         field,
@@ -747,8 +816,9 @@
         n,
         3,
     )
-    grads = swap_gather(to_degrees(synthesis, grad_by_order), n, False, 5)
-    coeff_orders, weight_grad = mix_back(blocks, grads, weights, mix_scale, 6)
+    coeff_orders, weight_grad = degree_exchange(
+        to_degrees(synthesis, grad_by_order), weights, n, mix_scale, 5, coeffs
+    )
     fourier_band = swap(to_latitudes(analysis, coeff_orders), n, False, False, 7)
     field_grad = final_field_grad(
         fourier_band, cotangent, jnp.asarray(np.ascontiguousarray(forward_np.T))

time: 140 us -> 134 us (0.957)
  Pallas kernels: 125 us -> 122 us
    pallas_call x2 -> x1, Pallas kernels: 29.5 us -> 19.8 us  [swap(): pl.pallas_call(functools.partial(plain_kernel, ex, None), out_shape=out,...]
    pallas_call x3 -> x2, Pallas kernels: 41.9 us -> 46.5 us  [degree_exchange(): pl.pallas_call(functools.partial(degree_kernel, n, backward, scale), out_...]
    pallas_call x1, Pallas kernels: 32.2 us -> 34.1 us  [response_exchange(): pl.pallas_call(functools.partial(response_kernel, ex), out_shape=(jax.Sha...]
    unnamed x20 -> x22, local copies, waits for them, and re-layouts: 7.54 us -> 6.76 us
where the time goes in v3:
time: 134 us; the launch traced here: 133 us
  Pallas kernels  122 us (91%)
  local copies, waits for them, and re-layouts  9.31 us (7%)
  matrix products  1.36 us (1%)
    pallas_call x2, Pallas kernels, degree_exchange(): pl.pallas_call(functools.partial(degree_kernel, n, backward, scale), out_...  46.5 us
    pallas_call x1, Pallas kernels, response_exchange(): pl.pallas_call(functools.partial(response_kernel, ex), out_shape=(jax.Sha...  34.1 us
    pallas_call x1, Pallas kernels, swap(): pl.pallas_call(functools.partial(plain_kernel, ex, None), out_shape=out,...  19.8 us
    pallas_call x1, Pallas kernels, fourier_exchange(): pl.pallas_call(functools.partial(fourier_kernel, ex, scale), out_shape=(j...  18.2 us
    unnamed x22, local copies, waits for them, and re-layouts  6.76 us
    pallas_call x1, Pallas kernels, final_field_grad(): pl.pallas_call(field_grad_kernel, grid=(held // 2,), out_shape=jax.ShapeD...  3.32 us

profile of v3, /device:TPU:8, one launch (start us, length us, event | category | flops | bytes accessed | tf_op | source)
XLA Modules:
  0.0 133.4 jit_solution(6162136606537107033)
XLA Ops:
  0.7 0.7 constant_dynamic-slice_fusion.log_start
  1.4 0.0 copy-start
  1.4 1.7 %copy-done = bf16[12,768,128]{2,1,0:T(8,128)(2,1)S(1)} copy-done((bf16[12,768,128]{2,1,0:T(8,128)(2,1)S(1)}, bf16[12,768,128]{2,1,0:T(8,128)(2,1)}, u32[]{:S(2)}) %copy-start) | copy-done | bytes 2359320
  3.1 0.0 copy-start.3
  3.1 1.1 copy-done.3
  4.2 0.0 copy-start.8
  4.2 1.0 copy-done.8
  5.2 0.0 copy-start.9
  5.2 0.7 copy-done.9
  5.8 0.0 copy-start.4
  5.8 18.2 %fourier_exchange.1 = (bf16[96,24,128]{2,1,0:T(8,128)(2,1)S(1)}, bf16[12,96,96]{2,1,0:T(8,128)(2,1)S(1)}, bf16[12,96,96]{2,1,0:T(8,128)(2,1)S(1)}, bf16[2,12,128,128]{3,2,1,0:T(8,128)(2,1)S(1)}) custom-call(bf16[12,768,128]{2,1,0:T(8,128)(2,1)S(1)} %copy-done, bf16[12,256,128]{2,1,0:T(8,128)(2,1)S(1)} %copy-done.3, bf16[192,768]{1,0:T(8,128)(2,1)S(1)} %copy-done.8, ...), custom_call_target="tpu_custom_call" | custom-call | tf_op jit(solution)/shard_map/fourier_exchange/pallas_call | solution.py:374
  24.0 0.0 copy-start.7
  24.0 0.3 fusion.2
  24.4 0.0 copy-start.1
  24.4 0.0 copy-start.2
  24.4 0.0 copy-start.6
  24.4 0.5 copy.13
  24.9 0.0 copy-done.4
  24.9 24.2 %degree_exchange.2 = (bf16[96,24,128]{2,1,0:T(8,128)(2,1)S(1)}, bf16[2,12,8,24,128]{4,3,2,1,0:T(8,128)(2,1)S(1)}) custom-call(bf16[96,24,128]{2,1,0:T(8,128)(2,1)S(1)} %bitcast.39, bf16[12,256,128]{2,1,0:T(8,128)(2,1)S(1)} %copy-done.4), custom_call_target="tpu_custom_call" | custom-call | tf_op jit(solution)/shard_map/degree_exchange/pallas_call | solution.py:747
  49.0 0.4 fusion
  49.4 0.5 copy.16
  49.9 0.0 copy-done.7
  49.9 0.0 copy-done.1
  49.9 0.0 copy-done.2
  49.9 0.0 copy-done.6
  49.9 34.1 %response_exchange.1 = (bf16[12,768,128]{2,1,0:T(8,128)(2,1)S(1)}, bf16[96,24,128]{2,1,0:T(8,128)(2,1)S(1)}) custom-call(bf16[96,24,128]{2,1,0:T(8,128)(2,1)S(1)} %bitcast.36, bf16[12,768,128]{2,1,0:T(8,128)(2,1)S(1)} %copy-done.1, bf16[12,768,128]{2,1,0:T(8,128)(2,1)S(1)} %copy-done.2, bf16[768,192]{1,0:T(8,128)(2,1)S(1)} %copy-done.6, ...), custom_call_target="tpu_custom_call" | custom-call | tf_op jit(solution)/shard_map/response_exchange/pallas_call | solution.py:500
  84.0 0.3 fusion.3
  84.3 0.5 copy.18
  84.8 22.3 %degree_exchange.3 = (bf16[96,24,128]{2,1,0:T(8,128)(2,1)S(1)}, bf16[12,256,128]{2,1,0:T(8,128)(2,1)S(1)}) custom-call(bf16[96,24,128]{2,1,0:T(8,128)(2,1)S(1)} %bitcast.37, bf16[2,12,128,128]{3,2,1,0:T(8,128)(2,1)S(1)} %get-tuple-element.19.refs_1_, bf16[2,12,8,24,128]{4,3,2,1,0:T(8,128)(2,1)S(1)} %get-tuple-element.20.refs_2_), custom_call_target="tpu_custom_call" | custom-call | tf_op jit(solution)/shard_map/degree_exchange/pallas_call | solution.py:747
  107.1 0.0 copy-start.5
  107.2 0.4 fusion.1
  107.5 0.5 copy.21
  108.0 19.8 %exchange.1.band = bf16[12,8,24,128]{3,2,1,0:T(8,128)(2,1)S(1)} custom-call(bf16[96,24,128]{2,1,0:T(8,128)(2,1)S(1)} %bitcast.38), custom_call_target="tpu_custom_call" | custom-call | tf_op jit(solution)/shard_map/exchange/pallas_call | solution.py:232
  127.8 0.0 copy-done.5
  127.8 3.3 %field_grad.1 = bf16[12,768,128]{2,1,0:T(8,128)(2,1)} custom-call(bf16[12,8,24,128]{3,2,1,0:T(8,128)(2,1)S(1)} %exchange.1.band, bf16[12,768,128]{2,1,0:T(8,128)(2,1)S(1)} %copy-done.2, bf16[768,192]{1,0:T(8,128)(2,1)S(1)} %copy-done.5), custom_call_target="tpu_custom_call" | custom-call | tf_op jit(solution)/shard_map/field_grad/pallas_call | solution.py:542
  131.2 1.4 %copy.40 = bf16[12,768,128]{2,1,0:T(8,128)(2,1)} copy(bf16[12,768,128]{2,1,0:T(8,128)(2,1)S(1)} %get-tuple-element.26) | data formatting | bytes 4718592
  132.6 0.9 copy.41
Async XLA Ops:
  1.4 1.7 %copy-start = (bf16[12,768,128]{2,1,0:T(8,128)(2,1)S(1)}, bf16[12,768,128]{2,1,0:T(8,128)(2,1)}, u32[]{:S(2)}) copy-start(bf16[12,768,128]{2,1,0:T(8,128)(2,1)} %field.3) | copy-start | bytes 7077892
  3.1 1.1 copy-start.3
  4.2 1.0 copy-start.8
  5.2 0.7 copy-start.9
  5.8 19.0 %copy-start.4 = (bf16[12,256,128]{2,1,0:T(8,128)(2,1)S(1)}, bf16[12,256,128]{2,1,0:T(8,128)(2,1)}, u32[]{:S(2)}) copy-start(bf16[12,256,128]{2,1,0:T(8,128)(2,1)} %refs_1_.1) | copy-start | bytes 2359300
  24.0 25.8 %copy-start.7 = (bf16[192,768]{1,0:T(8,128)(2,1)S(1)}, bf16[192,768]{1,0:T(8,128)(2,1)}, u32[]{:S(2)}) copy-start(bf16[192,768]{1,0:T(8,128)(2,1)} %constant.55.clone.inverse) | copy-start | bytes 884740
  24.4 25.5 %copy-start.1 = (bf16[12,768,128]{2,1,0:T(8,128)(2,1)S(1)}, bf16[12,768,128]{2,1,0:T(8,128)(2,1)}, u32[]{:S(2)}) copy-start(bf16[12,768,128]{2,1,0:T(8,128)(2,1)} %field.3) | copy-start | bytes 7077892
  24.4 25.5 %copy-start.2 = (bf16[12,768,128]{2,1,0:T(8,128)(2,1)S(1)}, bf16[12,768,128]{2,1,0:T(8,128)(2,1)}, u32[]{:S(2)}) copy-start(bf16[12,768,128]{2,1,0:T(8,128)(2,1)} %cotangent.3) | copy-start | bytes 7077892
  24.4 25.5 %copy-start.6 = (bf16[768,192]{1,0:T(8,128)(2,1)S(1)}, bf16[768,192]{1,0:T(8,128)(2,1)}, u32[]{:S(2)}) copy-start(bf16[768,192]{1,0:T(8,128)(2,1)} %constant.58.clone.inverse_t) | copy-start | bytes 884740
  107.1 20.7 %copy-start.5 = (bf16[768,192]{1,0:T(8,128)(2,1)S(1)}, bf16[768,192]{1,0:T(8,128)(2,1)}, u32[]{:S(2)}) copy-start(bf16[768,192]{1,0:T(8,128)(2,1)} %constant.59.clone.forward_t) | copy-start | bytes 884740

commit v4 on v3

--- a/solution.py
+++ b/solution.py
@@ -90,6 +90,13 @@
         self.n, self.held, self.spread, self.sparse = n, held, spread, sparse
 
     def greet(self, chan):
+        self.signal(chan)
+        self.hear(chan)
+
+    def hear(self, chan):
+        pl.semaphore_wait(pltpu.get_barrier_semaphore(), self.n - 1 + (1 if chan else 0))
+
+    def signal(self, chan):
         me = lax.axis_index("space")
         barrier = pltpu.get_barrier_semaphore()
         for k in range(1, self.n):
@@ -100,7 +107,6 @@
             pl.semaphore_signal(
                 barrier, inc=1, device_id={"chan": 1 - lax.axis_index("chan")}, device_id_type=MESH
             )
-        pl.semaphore_wait(barrier, self.n - 1 + (1 if chan else 0))
 
     def source(self, x, d):
         return x.at[:, d] if self.spread else x.at[pl.ds(d * self.held, self.held)]
@@ -151,11 +157,8 @@
                 copy.start() if start else copy.wait()
 
 
-def plain_kernel(ex, legendre, *refs):
-    if legendre is not None:
-        x, log_start, rows, y, analysis, synthesis, values = refs[:7]
-        send_sem, recv_sem, own_sem = refs[7:]
-    elif ex.sparse:
+def plain_kernel(ex, *refs):
+    if ex.sparse:
         x, y, zero, zero_sem, send_sem, recv_sem, own_sem = refs
     else:
         x, y, send_sem, recv_sem, own_sem = refs
@@ -167,9 +170,6 @@
     if ex.sparse:
         zero[...] = jnp.zeros_like(zero)
         zero_fill(ex, [y], zero, zero_sem, True)
-    if legendre is not None:
-        first_order = (ex.n - 1 - me) * ex.held
-        legendre_into(log_start, rows, legendre, first_order, values, analysis, synthesis)
     ex.when(me, own.wait)
     for k in range(1, ex.n):
         other, copy = ex.copy(x, y, k, send_sem, recv_sem, False)
@@ -191,13 +191,13 @@
     return pl.BlockSpec(memory_space=pltpu.VMEM)
 
 
-def params(collective_id):
+def params(collective_id, mebibytes=24):
     return pltpu.CompilerParams(
-        collective_id=collective_id, has_side_effects=True, vmem_limit_bytes=24 * 2**20
-    )
-
-
-def swap(x, n, spread, sparse, collective_id, legendre=None):
+        collective_id=collective_id, has_side_effects=True, vmem_limit_bytes=mebibytes * 2**20
+    )
+
+
+def swap(x, n, spread, sparse, collective_id):
     if spread:
         held, _, rows, width = x.shape
         shape = (n * held, rows, width)
@@ -212,25 +212,12 @@
         pltpu.SemaphoreType.DMA,
     ]
     out = jax.ShapeDtypeStruct(shape, x.dtype)
-    if legendre is not None:
-        log_start, rows_in, scale = legendre
-        orders, latitudes = log_start.shape
-        table = jax.ShapeDtypeStruct((orders, n * held, latitudes), jnp.bfloat16)
-        return pl.pallas_call(
-            functools.partial(plain_kernel, ex, scale),
-            out_shape=(out, table, table),
-            in_specs=[any_spec(), vmem_spec(), vmem_spec()],
-            out_specs=(any_spec(), vmem_spec(), vmem_spec()),
-            scratch_shapes=[pltpu.VMEM((orders, n * held, latitudes), jnp.float32)] + sems,
-            compiler_params=params(collective_id),
-            name="exchange_and_legendre",
-        )(x, log_start, rows_in)
     scratch = list(sems)
     if sparse:
         zeros = [pltpu.VMEM((held, rows, width), x.dtype), pltpu.SemaphoreType.DMA((1, n))]
         scratch = zeros + scratch
     return pl.pallas_call(
-        functools.partial(plain_kernel, ex, None),
+        functools.partial(plain_kernel, ex),
         out_shape=out,
         in_specs=[any_spec()],
         out_specs=any_spec(),
@@ -296,16 +283,18 @@
     synthesis_scale,
     field,
     weight,
-    forward,
-    log_start,
-    rows,
+    forward_in,
+    starts_in,
     y,
     analysis,
     synthesis,
     weights,
     values,
+    forward,
+    starts,
     held_field,
     bands,
+    table_sem,
     load_sem,
     send_sem,
     recv_sem,
@@ -322,9 +311,14 @@
         )
         for c in range(ch.chunks)
     ]
+    load_forward = pltpu.make_async_copy(forward_in, forward, table_sem.at[0])
+    load_starts = pltpu.make_async_copy(starts_in, starts, table_sem.at[1])
+    load_forward.start()
     for load in loads:
         load.start()
-    ex.greet(True)
+    load_starts.start()
+    ex.signal(True)
+    load_forward.wait()
     keep = pltpu.make_async_copy(
         weight.at[:, pl.ds(pl.multiple_of(chan * half, half), half)], weights.at[0], weight_sem.at[0]
     )
@@ -348,13 +342,24 @@
             return carry
 
         lax.fori_loop(0, CHUNK // 2, pair, 0)
+        if c == 0:
+            ex.hear(True)
         for k in range(1, n):
             ch.copy(bands, y, c, k, send_sem, recv_sem, True, True).start()
         ch.own(bands, y, c, own_sem, True).start()
     keep.start()
     give.start()
-    first_order = (n - 1 - order_block(me)) * analysis.shape[0]
-    legendre_into(log_start, rows, synthesis_scale, first_order, values, analysis, synthesis)
+    load_starts.wait()
+    block = n - 1 - order_block(me)
+    legendre_into(
+        starts.at[block],
+        starts.at[n],
+        synthesis_scale,
+        block * analysis.shape[0],
+        values,
+        analysis,
+        synthesis,
+    )
     for c in range(ch.chunks):
         ch.own(bands, y, c, own_sem, True).wait()
         for k in range(1, n):
@@ -364,9 +369,9 @@
     give.wait()
 
 
-def fourier_exchange(field, weight, forward, n, rows, log_start, rows_in, scale, collective_id):
+def fourier_exchange(field, weight, forward, n, rows, starts, scale, collective_id):
     held, longitudes, half = field.shape
-    orders, latitudes = log_start.shape
+    _, orders, latitudes = starts.shape
     degrees = weight.shape[0]
     ex = Exchange(n, held, True, False)
     chunks = held // CHUNK
@@ -379,21 +384,24 @@
             table,
             jax.ShapeDtypeStruct((2, degrees, half, half), field.dtype),
         ),
-        in_specs=[hbm_spec(), hbm_spec(), vmem_spec(), vmem_spec(), vmem_spec()],
+        in_specs=[hbm_spec()] * 4,
         out_specs=(any_spec(), vmem_spec(), vmem_spec(), any_spec()),
         scratch_shapes=[
             pltpu.VMEM((orders, degrees * n, latitudes), jnp.float32),
+            pltpu.VMEM(forward.shape, forward.dtype),
+            pltpu.VMEM(starts.shape, starts.dtype),
             pltpu.VMEM((held, longitudes, half), field.dtype),
             pltpu.VMEM((held, n, rows, half), field.dtype),
+            pltpu.SemaphoreType.DMA((2,)),
             pltpu.SemaphoreType.DMA((chunks,)),
             pltpu.SemaphoreType.DMA((chunks, n)),
             pltpu.SemaphoreType.DMA((chunks, n)),
             pltpu.SemaphoreType.DMA((chunks,)),
             pltpu.SemaphoreType.DMA((3,)),
         ],
-        compiler_params=params(collective_id),
+        compiler_params=params(collective_id, 60),
         name="fourier_exchange",
-    )(field, weight, forward, log_start, rows_in)
+    )(field, weight, forward, starts)
 
 
 TILE = 128
@@ -525,8 +533,20 @@
     )(grid, field, cotangent, inverse_t, inverse)
 
 
-def field_grad_kernel(band, cotangent, forward_t, out):
+def field_grad_kernel(
+    band, cotangent, forward_t, output, weight_grad, out, output_out, weight_out, sem
+):
     half = band.shape[-1]
+    passing = [
+        pltpu.make_async_copy(output, output_out, sem.at[0]),
+        pltpu.make_async_copy(weight_grad, weight_out, sem.at[1]),
+    ]
+
+    @pl.when(pl.program_id(0) == 0)
+    def _():
+        for copy in passing:
+            copy.start()
+
     for i in range(0, band.shape[0], 2):
         wide = jnp.concatenate([flat(band[i]), flat(band[i + 1])], axis=1)
         total = mm(forward_t[...], wide)
@@ -534,24 +554,34 @@
             part = total[:, side * half : (side + 1) * half]
             out[i + side] = (cotangent[i + side].astype(jnp.float32) + part).astype(out.dtype)
 
-
-def final_field_grad(band, cotangent, forward_t):
+    @pl.when(pl.program_id(0) == pl.num_programs(0) - 1)
+    def _():
+        for copy in passing:
+            copy.wait()
+
+
+def final_field_grad(band, cotangent, forward_t, output, weight_grad):
     held, n, rows, half = band.shape
     longitudes = cotangent.shape[1]
     lat = pl.BlockSpec((2, longitudes, half), lambda i: (i, 0, 0))
     return pl.pallas_call(
         field_grad_kernel,
         grid=(held // 2,),
-        out_shape=jax.ShapeDtypeStruct(cotangent.shape, cotangent.dtype),
+        out_shape=tuple(
+            jax.ShapeDtypeStruct(like.shape, like.dtype) for like in (cotangent, output, weight_grad)
+        ),
         in_specs=[
             pl.BlockSpec((2, n, rows, half), lambda i: (i, 0, 0, 0)),
             lat,
             pl.BlockSpec(forward_t.shape, lambda i: (0, 0)),
+            any_spec(),
+            any_spec(),
         ],
-        out_specs=lat,
+        out_specs=(lat, any_spec(), any_spec()),
+        scratch_shapes=[pltpu.SemaphoreType.DMA((2,))],
         compiler_params=pltpu.CompilerParams(vmem_limit_bytes=24 * 2**20),
         name="field_grad",
-    )(band, cotangent, forward_t)
+    )(band, cotangent, forward_t, output, weight_grad)
 
 
 def order_block(s):
@@ -782,16 +812,16 @@
     rows = 2 * orders_held
     mix_scale = 1.0 / math.sqrt(channels)
     chan = lax.axis_index("chan")
-    block = n - 1 - order_block(lax.axis_index("space"))
     held_blocks = [n - 1 - order_block(s) for s in range(n)]
     order_list = np.arange(degrees).reshape(n, orders_held)[held_blocks].reshape(-1)
     forward_np, inverse_np = fourier_tables(longitudes, order_list)
     forward, inverse = jnp.asarray(forward_np), jnp.asarray(inverse_np)
     log_np, rows_np, scale = latitude_rows(latitudes, longitudes, degrees)
-    log_start = lax.dynamic_slice_in_dim(jnp.asarray(log_np), block * orders_held, orders_held, 0)
-
+    last = np.zeros((1, orders_held, latitudes), np.float32)
+    last[0, :2] = rows_np
+    starts = np.concatenate([log_np.reshape(n, orders_held, latitudes), last])
     by_order, analysis, synthesis, weights = fourier_exchange(
-        field, spectral_weight, forward, n, rows, log_start, jnp.asarray(rows_np), scale, 0
+        field, spectral_weight, forward, n, rows, jnp.asarray(starts), scale, 0
     )
 
     def to_degrees(table, values):
@@ -820,8 +850,12 @@
         to_degrees(synthesis, grad_by_order), weights, n, mix_scale, 5, coeffs
     )
     fourier_band = swap(to_latitudes(analysis, coeff_orders), n, False, False, 7)
-    field_grad = final_field_grad(
-        fourier_band, cotangent, jnp.asarray(np.ascontiguousarray(forward_np.T))
+    field_grad, output, weight_grad = final_field_grad(
+        fourier_band,
+        cotangent,
+        jnp.asarray(np.ascontiguousarray(forward_np.T)),
+        output,
+        weight_grad,
     )
     return (output, field_grad, weight_grad)
 

time: 134 us -> 135 us (level)
  Pallas kernels: 122 us -> 130 us
  local copies, waits for them, and re-layouts: 9.31 us -> 2.2 us
    unnamed x22 -> x18, local copies, waits for them, and re-layouts: 6.76 us -> 0.38 us
    pallas_call x2, Pallas kernels: 46.5 us -> 52.5 us  [degree_exchange(): pl.pallas_call(functools.partial(degree_kernel, n, backward, scale), out_...]
where the time goes in v4:
time: 135 us
  Pallas kernels  130 us (96%)
  matrix products  2.57 us (2%)
  local copies, waits for them, and re-layouts  2.2 us (2%)
    pallas_call x2, Pallas kernels, degree_exchange(): pl.pallas_call(functools.partial(degree_kernel, n, backward, scale), out_...  52.5 us
    pallas_call x1, Pallas kernels, response_exchange(): pl.pallas_call(functools.partial(response_kernel, ex), out_shape=(jax.Sha...  34.1 us
    pallas_call x1, Pallas kernels, swap(): pl.pallas_call(functools.partial(plain_kernel, ex), out_shape=out, in_spe...  19.8 us
    pallas_call x1, Pallas kernels, fourier_exchange(): pl.pallas_call(functools.partial(fourier_kernel, ex, scale), out_shape=(j...  19.1 us
    pallas_call x1, Pallas kernels, final_field_grad(): pl.pallas_call(field_grad_kernel, grid=(held // 2,), out_shape=tuple((jax...  4.13 us

profile of v4, /device:TPU:8, one launch (start us, length us, event | category | flops | bytes accessed | tf_op | source)
XLA Modules:
  0.0 135.3 jit_solution(15019794102549601086)
XLA Ops:
  0.6 0.0 copy-start.2
  0.6 19.1 %fourier_exchange.1 = (bf16[96,24,128]{2,1,0:T(8,128)(2,1)}, bf16[12,96,96]{2,1,0:T(8,128)(2,1)}, bf16[12,96,96]{2,1,0:T(8,128)(2,1)}, bf16[2,12,128,128]{3,2,1,0:T(8,128)(2,1)}) custom-call(bf16[12,768,128]{2,1,0:T(8,128)(2,1)} %field.3, bf16[12,256,128]{2,1,0:T(8,128)(2,1)} %refs_1_.1, bf16[192,768]{1,0:T(8,128)(2,1)} %constant.10.clone.forward_in, ...), custom_call_target="tpu_custom_call" | custom-call | tf_op jit(solution)/shard_map/fourier_exchange/pallas_call | solution.py:379
  19.8 0.0 copy-start.8
  19.8 0.0 copy-start.6
  19.8 1.5 %fusion.2 = bf16[96,12,2,128]{3,0,2,1:T(8,128)(2,1)S(1)} fusion(bf16[96,12,2,128]{3,2,1,0:T(2,128)(2,1)} %bitcast.43, bf16[12,96,96]{2,1,0:T(8,128)(2,1)} %get-tuple-element.17), kind=kOutput, calls=%fused_computation.6 | convolution fusion | flops 56918016 | bytes 1400832 | tf_op jit(solution)/shard_map/mlj,jmrc->lmrc/dot_general | solution.py:802
  21.3 0.0 copy-start
  21.3 0.0 copy-start.1
  21.3 0.0 copy-start.5
  21.3 0.5 copy.12
  21.8 0.0 copy-done.2
  21.8 30.3 %degree_exchange.2 = (bf16[96,24,128]{2,1,0:T(8,128)(2,1)S(1)}, bf16[2,12,8,24,128]{4,3,2,1,0:T(8,128)(2,1)S(1)}) custom-call(bf16[96,24,128]{2,1,0:T(8,128)(2,1)S(1)} %bitcast.39, bf16[12,256,128]{2,1,0:T(8,128)(2,1)S(1)} %copy-done.2), custom_call_target="tpu_custom_call" | custom-call | tf_op jit(solution)/shard_map/degree_exchange/pallas_call | solution.py:777
  52.1 0.0 copy-done.8
  52.1 0.4 fusion
  52.5 0.5 copy.15
  52.9 0.0 copy-done.6
  53.0 0.0 copy-done
  53.0 0.0 copy-done.1
  53.0 0.0 copy-done.5
  53.0 34.1 %response_exchange.1 = (bf16[12,768,128]{2,1,0:T(8,128)(2,1)S(1)}, bf16[96,24,128]{2,1,0:T(8,128)(2,1)S(1)}) custom-call(bf16[96,24,128]{2,1,0:T(8,128)(2,1)S(1)} %bitcast.36, bf16[12,768,128]{2,1,0:T(8,128)(2,1)S(1)} %copy-done.1, bf16[12,768,128]{2,1,0:T(8,128)(2,1)S(1)} %copy-done, bf16[768,192]{1,0:T(8,128)(2,1)S(1)} %copy-done.5, ...), custom_call_target="tpu_custom_call" | custom-call | tf_op jit(solution)/shard_map/response_exchange/pallas_call | solution.py:508
  87.1 0.0 copy-start.3
  87.1 0.0 copy-start.7
  87.1 0.3 fusion.3
  87.4 0.5 copy.17
  87.9 0.3 copy-done.3
  88.2 22.2 %degree_exchange.3 = (bf16[96,24,128]{2,1,0:T(8,128)(2,1)S(1)}, bf16[12,256,128]{2,1,0:T(8,128)(2,1)S(1)}) custom-call(bf16[96,24,128]{2,1,0:T(8,128)(2,1)S(1)} %bitcast.37, bf16[2,12,128,128]{3,2,1,0:T(8,128)(2,1)S(1)} %copy-done.3, bf16[2,12,8,24,128]{4,3,2,1,0:T(8,128)(2,1)S(1)} %get-tuple-element.22.refs_2_), custom_call_target="tpu_custom_call" | custom-call | tf_op jit(solution)/shard_map/degree_exchange/pallas_call | solution.py:777
  110.5 0.0 copy-start.4
  110.5 0.0 copy-done.7
  110.5 0.4 fusion.1
  110.9 0.5 copy.20
  111.3 19.8 %exchange.1.band = bf16[12,8,24,128]{3,2,1,0:T(8,128)(2,1)S(1)} custom-call(bf16[96,24,128]{2,1,0:T(8,128)(2,1)S(1)} %bitcast.38), custom_call_target="tpu_custom_call" | custom-call | tf_op jit(solution)/shard_map/exchange/pallas_call | solution.py:219
  131.2 0.0 copy-done.4
  131.2 4.1 %field_grad.1 = (bf16[12,768,128]{2,1,0:T(8,128)(2,1)}, bf16[12,768,128]{2,1,0:T(8,128)(2,1)}, bf16[12,256,128]{2,1,0:T(8,128)(2,1)}) custom-call(bf16[12,8,24,128]{3,2,1,0:T(8,128)(2,1)S(1)} %exchange.1.band, bf16[12,768,128]{2,1,0:T(8,128)(2,1)S(1)} %copy-done, bf16[768,192]{1,0:T(8,128)(2,1)S(1)} %copy-done.4, ...), custom_call_target="tpu_custom_call" | custom-call | tf_op jit(solution)/shard_map/field_grad/pallas_call | solution.py:567
Async XLA Ops:
  0.6 21.2 %copy-start.2 = (bf16[12,256,128]{2,1,0:T(8,128)(2,1)S(1)}, bf16[12,256,128]{2,1,0:T(8,128)(2,1)}, u32[]{:S(2)}) copy-start(bf16[12,256,128]{2,1,0:T(8,128)(2,1)} %refs_1_.1) | copy-start | bytes 2359300
  19.8 32.3 %copy-start.8 = (bf16[12,96,96]{2,1,0:T(8,128)(2,1)S(1)}, bf16[12,96,96]{2,1,0:T(8,128)(2,1)}, u32[]{:S(2)}) copy-start(bf16[12,96,96]{2,1,0:T(8,128)(2,1)} %get-tuple-element.19) | copy-start | bytes 663556
  19.8 33.2 %copy-start.6 = (bf16[192,768]{1,0:T(8,128)(2,1)S(1)}, bf16[192,768]{1,0:T(8,128)(2,1)}, u32[]{:S(2)}) copy-start(bf16[192,768]{1,0:T(8,128)(2,1)} %constant.11.clone.inverse) | copy-start | bytes 884740
  21.3 31.7 %copy-start = (bf16[12,768,128]{2,1,0:T(8,128)(2,1)S(1)}, bf16[12,768,128]{2,1,0:T(8,128)(2,1)}, u32[]{:S(2)}) copy-start(bf16[12,768,128]{2,1,0:T(8,128)(2,1)} %cotangent.3) | copy-start | bytes 7077892
  21.3 31.7 %copy-start.1 = (bf16[12,768,128]{2,1,0:T(8,128)(2,1)S(1)}, bf16[12,768,128]{2,1,0:T(8,128)(2,1)}, u32[]{:S(2)}) copy-start(bf16[12,768,128]{2,1,0:T(8,128)(2,1)} %field.3) | copy-start | bytes 7077892
  21.3 31.7 %copy-start.5 = (bf16[768,192]{1,0:T(8,128)(2,1)S(1)}, bf16[768,192]{1,0:T(8,128)(2,1)}, u32[]{:S(2)}) copy-start(bf16[768,192]{1,0:T(8,128)(2,1)} %constant.13.clone.inverse_t) | copy-start | bytes 884740
  87.1 1.1 copy-start.3
  87.1 23.4 %copy-start.7 = (bf16[12,96,96]{2,1,0:T(8,128)(2,1)S(1)}, bf16[12,96,96]{2,1,0:T(8,128)(2,1)}, u32[]{:S(2)}) copy-start(bf16[12,96,96]{2,1,0:T(8,128)(2,1)} %get-tuple-element.17) | copy-start | bytes 663556
  110.5 20.7 %copy-start.4 = (bf16[768,192]{1,0:T(8,128)(2,1)S(1)}, bf16[768,192]{1,0:T(8,128)(2,1)}, u32[]{:S(2)}) copy-start(bf16[768,192]{1,0:T(8,128)(2,1)} %constant.14.clone.forward_t) | copy-start | bytes 884740

commit v5 on v4

--- a/solution.py
+++ b/solution.py
@@ -528,7 +528,7 @@
             pltpu.SemaphoreType.DMA((chunks,)),
             pltpu.SemaphoreType.DMA((chunks,)),
         ],
-        compiler_params=params(collective_id),
+        compiler_params=params(collective_id, 60),
         name="response_exchange",
     )(grid, field, cotangent, inverse_t, inverse)
 

time: 135 us -> 138 us (1.022)
  no operation moved by 1% of the time
where the time goes in v5:
time: 138 us
  Pallas kernels  131 us (95%)
  matrix products  3.7 us (3%)
  local copies, waits for them, and re-layouts  2.67 us (2%)
    pallas_call x2, Pallas kernels, degree_exchange(): pl.pallas_call(functools.partial(degree_kernel, n, backward, scale), out_...  52.6 us
    pallas_call x1, Pallas kernels, response_exchange(): pl.pallas_call(functools.partial(response_kernel, ex), out_shape=(jax.Sha...  35.1 us
    pallas_call x1, Pallas kernels, swap(): pl.pallas_call(functools.partial(plain_kernel, ex), out_shape=out, in_spe...  19.8 us
    pallas_call x1, Pallas kernels, fourier_exchange(): pl.pallas_call(functools.partial(fourier_kernel, ex, scale), out_shape=(j...  19.1 us
    pallas_call x1, Pallas kernels, final_field_grad(): pl.pallas_call(field_grad_kernel, grid=(held // 2,), out_shape=tuple((jax...  4.14 us
    dot_general x4, matrix products, dot32(): return jnp.einsum(formula, left, right, preferred_element_type=jnp.float32)  3.7 us

profile of v5, /device:TPU:8, one launch (start us, length us, event | category | flops | bytes accessed | tf_op | source)
XLA Modules:
  0.0 138.0 jit_solution(4714434611187211305)
XLA Ops:
  0.6 0.0 copy-start.1
  0.6 19.1 %fourier_exchange.1 = (bf16[96,24,128]{2,1,0:T(8,128)(2,1)}, bf16[12,96,96]{2,1,0:T(8,128)(2,1)}, bf16[12,96,96]{2,1,0:T(8,128)(2,1)}, bf16[2,12,128,128]{3,2,1,0:T(8,128)(2,1)}) custom-call(bf16[12,768,128]{2,1,0:T(8,128)(2,1)} %field.3, bf16[12,256,128]{2,1,0:T(8,128)(2,1)} %refs_1_.1, bf16[192,768]{1,0:T(8,128)(2,1)} %constant.10.clone.forward_in, ...), custom_call_target="tpu_custom_call" | custom-call | tf_op jit(solution)/shard_map/fourier_exchange/pallas_call | solution.py:379
  19.7 0.0 copy-start.6
  19.8 1.5 %fusion.2 = bf16[96,12,2,128]{3,0,2,1:T(8,128)(2,1)S(1)} fusion(bf16[96,12,2,128]{3,2,1,0:T(2,128)(2,1)} %bitcast.42, bf16[12,96,96]{2,1,0:T(8,128)(2,1)} %get-tuple-element.17), kind=kOutput, calls=%fused_computation.6 | convolution fusion | flops 56918016 | bytes 1400832 | tf_op jit(solution)/shard_map/mlj,jmrc->lmrc/dot_general | solution.py:802
  21.3 0.5 copy.12
  21.7 0.0 copy-done.1
  21.7 30.3 %degree_exchange.2 = (bf16[96,24,128]{2,1,0:T(8,128)(2,1)S(1)}, bf16[2,12,8,24,128]{4,3,2,1,0:T(8,128)(2,1)S(1)}) custom-call(bf16[96,24,128]{2,1,0:T(8,128)(2,1)S(1)} %bitcast.38, bf16[12,256,128]{2,1,0:T(8,128)(2,1)S(1)} %copy-done.1), custom_call_target="tpu_custom_call" | custom-call | tf_op jit(solution)/shard_map/degree_exchange/pallas_call | solution.py:777
  52.0 0.0 copy-done.6
  52.0 0.4 fusion
  52.4 1.3 copy.15
  53.7 35.1 %response_exchange.1 = (bf16[12,768,128]{2,1,0:T(8,128)(2,1)}, bf16[96,24,128]{2,1,0:T(8,128)(2,1)}) custom-call(bf16[96,24,128]{2,1,0:T(8,128)(2,1)} %bitcast.41, bf16[12,768,128]{2,1,0:T(8,128)(2,1)} %field.3, bf16[12,768,128]{2,1,0:T(8,128)(2,1)} %cotangent.3, bf16[768,192]{1,0:T(8,128)(2,1)} %constant.13.clone.inverse_t, ...), custom_call_target="tpu_custom_call" | custom-call | tf_op jit(solution)/shard_map/response_exchange/pallas_call | solution.py:508
  88.8 0.0 copy-start.3
  88.8 0.0 copy-start.5
  88.8 1.5 %fusion.3 = bf16[96,12,2,128]{3,0,2,1:T(8,128)(2,1)S(1)} fusion(bf16[96,12,2,128]{3,2,1,0:T(2,128)(2,1)} %bitcast.43, bf16[12,96,96]{2,1,0:T(8,128)(2,1)S(1)} %copy-done.6), kind=kOutput, calls=%fused_computation.7 | convolution fusion | flops 56918016 | bytes 1400832 | tf_op jit(solution)/shard_map/mlj,jmrc->lmrc/dot_general | solution.py:802
  90.3 0.5 copy.17
  90.7 0.0 copy-done.3
  90.7 0.0 copy-start.2
  90.8 22.3 %degree_exchange.3 = (bf16[96,24,128]{2,1,0:T(8,128)(2,1)S(1)}, bf16[12,256,128]{2,1,0:T(8,128)(2,1)S(1)}) custom-call(bf16[96,24,128]{2,1,0:T(8,128)(2,1)S(1)} %bitcast.36, bf16[2,12,128,128]{3,2,1,0:T(8,128)(2,1)S(1)} %copy-done.3, bf16[2,12,8,24,128]{4,3,2,1,0:T(8,128)(2,1)S(1)} %get-tuple-element.22.refs_2_), custom_call_target="tpu_custom_call" | custom-call | tf_op jit(solution)/shard_map/degree_exchange/pallas_call | solution.py:777
  113.1 0.0 copy-start
  113.1 0.0 copy-start.4
  113.1 0.0 copy-done.5
  113.1 0.4 fusion.1
  113.5 0.5 copy.20
  114.0 19.8 %exchange.1.band = bf16[12,8,24,128]{3,2,1,0:T(8,128)(2,1)S(1)} custom-call(bf16[96,24,128]{2,1,0:T(8,128)(2,1)S(1)} %bitcast.37), custom_call_target="tpu_custom_call" | custom-call | tf_op jit(solution)/shard_map/exchange/pallas_call | solution.py:219
  133.8 0.0 copy-done.2
  133.8 0.0 copy-done
  133.8 0.0 copy-done.4
  133.8 4.1 %field_grad.1 = (bf16[12,768,128]{2,1,0:T(8,128)(2,1)}, bf16[12,768,128]{2,1,0:T(8,128)(2,1)}, bf16[12,256,128]{2,1,0:T(8,128)(2,1)}) custom-call(bf16[12,8,24,128]{3,2,1,0:T(8,128)(2,1)S(1)} %exchange.1.band, bf16[12,768,128]{2,1,0:T(8,128)(2,1)S(1)} %copy-done, bf16[768,192]{1,0:T(8,128)(2,1)S(1)} %copy-done.4, bf16[12,768,128]{2,1,0:T(8,128)(2,1)S(1)} %copy-done.2, ...), custom_call_target="tpu_custom_call" | custom-call | tf_op jit(solution)/shard_map/field_grad/pallas_call | solution.py:567
Async XLA Ops:
  0.6 21.1 %copy-start.1 = (bf16[12,256,128]{2,1,0:T(8,128)(2,1)S(1)}, bf16[12,256,128]{2,1,0:T(8,128)(2,1)}, u32[]{:S(2)}) copy-start(bf16[12,256,128]{2,1,0:T(8,128)(2,1)} %refs_1_.1) | copy-start | bytes 2359300
  19.7 32.3 %copy-start.6 = (bf16[12,96,96]{2,1,0:T(8,128)(2,1)S(1)}, bf16[12,96,96]{2,1,0:T(8,128)(2,1)}, u32[]{:S(2)}) copy-start(bf16[12,96,96]{2,1,0:T(8,128)(2,1)} %get-tuple-element.19) | copy-start | bytes 663556
  88.8 2.0 %copy-start.3 = (bf16[2,12,128,128]{3,2,1,0:T(8,128)(2,1)S(1)}, bf16[2,12,128,128]{3,2,1,0:T(8,128)(2,1)}, u32[]{:S(2)}) copy-start(bf16[2,12,128,128]{3,2,1,0:T(8,128)(2,1)} %get-tuple-element.21.refs_1_) | copy-start | bytes 2359300
  88.8 24.3 %copy-start.5 = (bf16[12,96,96]{2,1,0:T(8,128)(2,1)S(1)}, bf16[12,96,96]{2,1,0:T(8,128)(2,1)}, u32[]{:S(2)}) copy-start(bf16[12,96,96]{2,1,0:T(8,128)(2,1)} %get-tuple-element.17) | copy-start | bytes 663556
  90.7 43.1 %copy-start.2 = (bf16[12,768,128]{2,1,0:T(8,128)(2,1)S(1)}, bf16[12,768,128]{2,1,0:T(8,128)(2,1)}, u32[]{:S(2)}) copy-start(bf16[12,768,128]{2,1,0:T(8,128)(2,1)} %get-tuple-element.24.output) | copy-start | bytes 7077892
  113.1 20.7 %copy-start = (bf16[12,768,128]{2,1,0:T(8,128)(2,1)S(1)}, bf16[12,768,128]{2,1,0:T(8,128)(2,1)}, u32[]{:S(2)}) copy-start(bf16[12,768,128]{2,1,0:T(8,128)(2,1)} %cotangent.3) | copy-start | bytes 7077892
  113.1 20.7 %copy-start.4 = (bf16[768,192]{1,0:T(8,128)(2,1)S(1)}, bf16[768,192]{1,0:T(8,128)(2,1)}, u32[]{:S(2)}) copy-start(bf16[768,192]{1,0:T(8,128)(2,1)} %constant.14.clone.forward_t) | copy-start | bytes 884740

commit v6 on v4

--- a/solution.py
+++ b/solution.py
@@ -399,7 +399,7 @@
             pltpu.SemaphoreType.DMA((chunks,)),
             pltpu.SemaphoreType.DMA((3,)),
         ],
-        compiler_params=params(collective_id, 60),
+        compiler_params=params(collective_id),
         name="fourier_exchange",
     )(field, weight, forward, starts)
 

time: 135 us -> 131 us (0.970)
  Pallas kernels: 130 us -> 122 us
  local copies, waits for them, and re-layouts: 2.2 us -> 6.5 us
    pallas_call x2, Pallas kernels: 52.5 us -> 46.5 us  [degree_exchange(): pl.pallas_call(functools.partial(degree_kernel, n, backward, scale), out_...]
    unnamed x18 -> x20, local copies, waits for them, and re-layouts: 0.38 us -> 4.67 us
where the time goes in v6:
time: 131 us
  Pallas kernels  122 us (93%)
  local copies, waits for them, and re-layouts  6.5 us (5%)
  matrix products  1.36 us (1%)
    pallas_call x2, Pallas kernels, degree_exchange(): pl.pallas_call(functools.partial(degree_kernel, n, backward, scale), out_...  46.5 us
    pallas_call x1, Pallas kernels, response_exchange(): pl.pallas_call(functools.partial(response_kernel, ex), out_shape=(jax.Sha...  34.1 us
    pallas_call x1, Pallas kernels, swap(): pl.pallas_call(functools.partial(plain_kernel, ex), out_shape=out, in_spe...  19.8 us
    pallas_call x1, Pallas kernels, fourier_exchange(): pl.pallas_call(functools.partial(fourier_kernel, ex, scale), out_shape=(j...  17.8 us
    unnamed x20, local copies, waits for them, and re-layouts  4.67 us
    pallas_call x1, Pallas kernels, final_field_grad(): pl.pallas_call(field_grad_kernel, grid=(held // 2,), out_shape=tuple((jax...  4.13 us

profile of v6, /device:TPU:8, one launch (start us, length us, event | category | flops | bytes accessed | tf_op | source)
XLA Modules:
  0.0 131.0 jit_solution(3722687019633121346)
XLA Ops:
  0.6 0.0 copy-start.1
  0.6 1.7 %copy-done.1 = bf16[12,768,128]{2,1,0:T(8,128)(2,1)S(1)} copy-done((bf16[12,768,128]{2,1,0:T(8,128)(2,1)S(1)}, bf16[12,768,128]{2,1,0:T(8,128)(2,1)}, u32[]{:S(2)}) %copy-start.1) | copy-done | bytes 2359320
  2.3 0.0 copy-start.3
  2.3 1.1 copy-done.3
  3.4 0.0 copy-start.8
  3.4 1.0 copy-done.8
  4.4 0.0 copy-start.9
  4.4 0.9 copy-done.9
  5.3 0.0 copy-start.4
  5.3 17.8 %fourier_exchange.1 = (bf16[96,24,128]{2,1,0:T(8,128)(2,1)S(1)}, bf16[12,96,96]{2,1,0:T(8,128)(2,1)S(1)}, bf16[12,96,96]{2,1,0:T(8,128)(2,1)S(1)}, bf16[2,12,128,128]{3,2,1,0:T(8,128)(2,1)S(1)}) custom-call(bf16[12,768,128]{2,1,0:T(8,128)(2,1)S(1)} %copy-done.1, bf16[12,256,128]{2,1,0:T(8,128)(2,1)S(1)} %copy-done.3, bf16[192,768]{1,0:T(8,128)(2,1)S(1)} %copy-done.8, ...), custom_call_target="tpu_custom_call" | custom-call | tf_op jit(solution)/shard_map/fourier_exchange/pallas_call | solution.py:379
  23.1 0.0 copy-start.7
  23.1 0.3 fusion.2
  23.4 0.0 copy-start
  23.4 0.0 copy-start.2
  23.4 0.0 copy-start.6
  23.4 0.5 copy.12
  23.9 0.0 copy-done.4
  23.9 24.2 %degree_exchange.2 = (bf16[96,24,128]{2,1,0:T(8,128)(2,1)S(1)}, bf16[2,12,8,24,128]{4,3,2,1,0:T(8,128)(2,1)S(1)}) custom-call(bf16[96,24,128]{2,1,0:T(8,128)(2,1)S(1)} %bitcast.39, bf16[12,256,128]{2,1,0:T(8,128)(2,1)S(1)} %copy-done.4), custom_call_target="tpu_custom_call" | custom-call | tf_op jit(solution)/shard_map/degree_exchange/pallas_call | solution.py:777
  48.1 0.4 fusion
  48.4 0.5 copy.15
  48.9 0.0 copy-done.7
  48.9 0.0 copy-done
  48.9 0.0 copy-done.2
  48.9 0.0 copy-done.6
  48.9 34.1 %response_exchange.1 = (bf16[12,768,128]{2,1,0:T(8,128)(2,1)S(1)}, bf16[96,24,128]{2,1,0:T(8,128)(2,1)S(1)}) custom-call(bf16[96,24,128]{2,1,0:T(8,128)(2,1)S(1)} %bitcast.36, bf16[12,768,128]{2,1,0:T(8,128)(2,1)S(1)} %copy-done.2, bf16[12,768,128]{2,1,0:T(8,128)(2,1)S(1)} %copy-done, bf16[768,192]{1,0:T(8,128)(2,1)S(1)} %copy-done.6, ...), custom_call_target="tpu_custom_call" | custom-call | tf_op jit(solution)/shard_map/response_exchange/pallas_call | solution.py:508
  83.0 0.3 fusion.3
  83.4 0.5 copy.17
  83.8 22.3 %degree_exchange.3 = (bf16[96,24,128]{2,1,0:T(8,128)(2,1)S(1)}, bf16[12,256,128]{2,1,0:T(8,128)(2,1)S(1)}) custom-call(bf16[96,24,128]{2,1,0:T(8,128)(2,1)S(1)} %bitcast.37, bf16[2,12,128,128]{3,2,1,0:T(8,128)(2,1)S(1)} %get-tuple-element.21.refs_1_, bf16[2,12,8,24,128]{4,3,2,1,0:T(8,128)(2,1)S(1)} %get-tuple-element.22.refs_2_), custom_call_target="tpu_custom_call" | custom-call | tf_op jit(solution)/shard_map/degree_exchange/pallas_call | solution.py:777
  106.2 0.0 copy-start.5
  106.2 0.4 fusion.1
  106.5 0.5 copy.20
  107.0 19.8 %exchange.1.band = bf16[12,8,24,128]{3,2,1,0:T(8,128)(2,1)S(1)} custom-call(bf16[96,24,128]{2,1,0:T(8,128)(2,1)S(1)} %bitcast.38), custom_call_target="tpu_custom_call" | custom-call | tf_op jit(solution)/shard_map/exchange/pallas_call | solution.py:219
  126.8 0.0 copy-done.5
  126.8 4.1 %field_grad.1 = (bf16[12,768,128]{2,1,0:T(8,128)(2,1)}, bf16[12,768,128]{2,1,0:T(8,128)(2,1)}, bf16[12,256,128]{2,1,0:T(8,128)(2,1)}) custom-call(bf16[12,8,24,128]{3,2,1,0:T(8,128)(2,1)S(1)} %exchange.1.band, bf16[12,768,128]{2,1,0:T(8,128)(2,1)S(1)} %copy-done, bf16[768,192]{1,0:T(8,128)(2,1)S(1)} %copy-done.5, ...), custom_call_target="tpu_custom_call" | custom-call | tf_op jit(solution)/shard_map/field_grad/pallas_call | solution.py:567
Async XLA Ops:
  0.6 1.7 %copy-start.1 = (bf16[12,768,128]{2,1,0:T(8,128)(2,1)S(1)}, bf16[12,768,128]{2,1,0:T(8,128)(2,1)}, u32[]{:S(2)}) copy-start(bf16[12,768,128]{2,1,0:T(8,128)(2,1)} %field.3) | copy-start | bytes 7077892
  2.3 1.1 copy-start.3
  3.4 1.0 copy-start.8
  4.4 0.9 copy-start.9
  5.3 18.6 %copy-start.4 = (bf16[12,256,128]{2,1,0:T(8,128)(2,1)S(1)}, bf16[12,256,128]{2,1,0:T(8,128)(2,1)}, u32[]{:S(2)}) copy-start(bf16[12,256,128]{2,1,0:T(8,128)(2,1)} %refs_1_.1) | copy-start | bytes 2359300
  23.1 25.8 %copy-start.7 = (bf16[192,768]{1,0:T(8,128)(2,1)S(1)}, bf16[192,768]{1,0:T(8,128)(2,1)}, u32[]{:S(2)}) copy-start(bf16[192,768]{1,0:T(8,128)(2,1)} %constant.11.clone.inverse) | copy-start | bytes 884740
  23.4 25.5 %copy-start = (bf16[12,768,128]{2,1,0:T(8,128)(2,1)S(1)}, bf16[12,768,128]{2,1,0:T(8,128)(2,1)}, u32[]{:S(2)}) copy-start(bf16[12,768,128]{2,1,0:T(8,128)(2,1)} %cotangent.3) | copy-start | bytes 7077892
  23.4 25.5 %copy-start.2 = (bf16[12,768,128]{2,1,0:T(8,128)(2,1)S(1)}, bf16[12,768,128]{2,1,0:T(8,128)(2,1)}, u32[]{:S(2)}) copy-start(bf16[12,768,128]{2,1,0:T(8,128)(2,1)} %field.3) | copy-start | bytes 7077892
  23.4 25.5 %copy-start.6 = (bf16[768,192]{1,0:T(8,128)(2,1)S(1)}, bf16[768,192]{1,0:T(8,128)(2,1)}, u32[]{:S(2)}) copy-start(bf16[768,192]{1,0:T(8,128)(2,1)} %constant.13.clone.inverse_t) | copy-start | bytes 884740
  106.2 20.7 %copy-start.5 = (bf16[768,192]{1,0:T(8,128)(2,1)S(1)}, bf16[768,192]{1,0:T(8,128)(2,1)}, u32[]{:S(2)}) copy-start(bf16[768,192]{1,0:T(8,128)(2,1)} %constant.14.clone.forward_t) | copy-start | bytes 884740
